TPU v7x, 256 devices: a whole 4x4x8 slice. The times are simulated.
256 devices in a mesh: ctx: 64 (over z, y_hi, x), tp: 4 (over y_lo, core).
Axes of the slice: x: 4, y: 4 (y_hi: 2, y_lo: 2; y = y_hi * 2 + y_lo), z: 8, core: 2. Of those that a mesh axis runs over, the one named last changes fastest.
Arguments:
- queries: bfloat16 [8192, 8192], P(('ctx', 'tp')), may hold values from -200 to 200
- key_head_states: bfloat16 [8192, 1024], P(('ctx', 'tp')), may hold values from -6 to 6
- value_head_states: bfloat16 [8192, 1024], P(('ctx', 'tp')), may hold values from -6 to 6
- output_gradient: bfloat16 [8192, 8192], P(('ctx', 'tp')), may hold values from -6 to 6
- doc_starts: int32 [16], replicated, may hold values from 0 to 8191, as said below
- span_map: int32 [128], replicated, may hold values from 0 to 127, as said below
Outputs:
- query_grad: bfloat16 [8192, 8192], P(('ctx', 'tp'))
- key_grad: bfloat16 [8192, 1024], P(('ctx', 'tp'))
- value_grad: bfloat16 [8192, 1024], P(('ctx', 'tp'))
Inputs may be any that keep to these rules, and one draw needn't show every extreme that they name: `span_map`: entries 2c and 2c + 1 are the spans held in row block c of 128 rows: a mirrored pair m and 127 - m with m < 64. Every span appears once. `doc_starts`: strictly increasing, the first is 0. The sequence is four stretches of 2048 positions that no document crosses; one stretch is a single document, each other stretch holds five.
All inputs are finite; a program needn't handle non-finite values.
Results may differ from a plain program's by a relative error of at most 0.0075.
Values may be sent and summed in bfloat16 or wider, within the bound.
A program may use at most 128 MiB of HBM per device.

v0:
```python
import math

import jax
import jax.numpy as jnp
from jax import lax
from jax.sharding import PartitionSpec as P

QUERY_HEADS = 64
KEY_VALUE_HEADS = 8
HEAD_WIDTH = 128


NEG_BIG = -1e30


def doc_number(positions, doc_starts):
    covered = (positions[:, None] >= doc_starts[None, :]).astype(jnp.int32)
    return jnp.sum(covered, axis=1) - 1


def fetch_keys(key_local, value_local):
    return (
        lax.all_gather(key_local, "ctx", axis=0, tiled=True),
        lax.all_gather(value_local, "ctx", axis=0, tiled=True),
    )


def tile_scores(query_rows, key_block, softmax_scale):
    return (
        jnp.einsum("tgjd,kgd->tgjk", query_rows, key_block, preferred_element_type=jnp.float32)
        * softmax_scale
    )


def allowed_pairs(query_pos, query_doc, key_pos, key_doc):
    same_doc = (query_doc[:, None] == key_doc[None, :]) & (key_pos[None, :] <= query_pos[:, None])
    return same_doc[:, None, None, :]


def tile_grads(span_data, key_block, value_block, key_pos, key_doc, softmax_scale):
    query_rows, grad_rows, query_pos, query_doc, first_block, last_block, log_total, row_delta = (
        span_data
    )
    scores = tile_scores(query_rows, key_block, softmax_scale)
    allowed = allowed_pairs(query_pos, query_doc, key_pos, key_doc)
    weights = jnp.where(allowed, jnp.exp(scores - log_total[..., None]), 0.0)
    dweights = jnp.einsum(
        "tgjd,kgd->tgjk", grad_rows, value_block, preferred_element_type=jnp.float32
    )
    dscores = weights * (dweights - row_delta[..., None])
    return (weights.astype(jnp.bfloat16), dscores.astype(jnp.bfloat16))


def span_stats(
    query_rows,
    grad_rows,
    query_pos,
    query_doc,
    key_global,
    value_global,
    key_pos,
    key_doc,
    first_block,
    last_block,
    block_rows,
    softmax_scale,
):
    stat_shape = query_rows.shape[:3]

    def span_block_step(block_id, carry):
        running_max, running_sum, running_dot = carry
        block_begin = block_id * block_rows
        key_block = lax.dynamic_slice_in_dim(key_global, block_begin, block_rows, 0)
        value_block = lax.dynamic_slice_in_dim(value_global, block_begin, block_rows, 0)
        block_pos = lax.dynamic_slice_in_dim(key_pos, block_begin, block_rows, 0)
        block_doc = lax.dynamic_slice_in_dim(key_doc, block_begin, block_rows, 0)
        scores = tile_scores(query_rows, key_block, softmax_scale)
        allowed = allowed_pairs(query_pos, query_doc, block_pos, block_doc)
        masked = jnp.where(allowed, scores, NEG_BIG)
        new_max = jnp.maximum(running_max, jnp.max(masked, axis=-1))
        factor = jnp.exp(running_max - new_max)
        exponent = jnp.where(allowed, jnp.exp(masked - new_max[..., None]), 0.0)
        dweights = jnp.einsum(
            "tgjd,kgd->tgjk", grad_rows, value_block, preferred_element_type=jnp.float32
        )
        running_sum = running_sum * factor + jnp.sum(exponent, axis=-1)
        running_dot = running_dot * factor + jnp.sum(exponent * dweights, axis=-1)
        return (new_max, running_sum, running_dot)

    initial_state = (
        jnp.full(stat_shape, NEG_BIG, jnp.float32),
        jnp.zeros(stat_shape, jnp.float32),
        jnp.zeros(stat_shape, jnp.float32),
    )
    final_max, final_sum, final_dot = lax.fori_loop(
        first_block, last_block, span_block_step, initial_state
    )
    return (final_max + jnp.log(final_sum), final_dot / final_sum)


def shards(queries, key_head_states, value_head_states, output_gradient, doc_starts, span_map):
    query_local, grad_local, key_local, value_local = (
        lax.all_to_all(queries, "tp", split_axis=1, concat_axis=0, tiled=True),
        lax.all_to_all(output_gradient, "tp", split_axis=1, concat_axis=0, tiled=True),
        lax.all_to_all(key_head_states, "tp", split_axis=1, concat_axis=0, tiled=True),
        lax.all_to_all(value_head_states, "tp", split_axis=1, concat_axis=0, tiled=True),
    )
    key_all, value_all = fetch_keys(key_local, value_local)
    tok_rows = query_local.shape[0]
    span_rows = tok_rows // 2
    kv_local = key_local.shape[1] // HEAD_WIDTH
    query_group_count = QUERY_HEADS // KEY_VALUE_HEADS
    total_rows = key_all.shape[0]
    slot_count = span_map.shape[0]
    softmax_scale = 1.0 / math.sqrt(HEAD_WIDTH)
    block_rows = min(512, total_rows)
    slot_ids = jnp.arange(slot_count, dtype=jnp.int32)
    slot_of_span = jnp.sum(
        jnp.where(span_map[None, :] == slot_ids[:, None], slot_ids[None, :], 0), axis=1
    )
    key_global = key_all.reshape(slot_count, span_rows, kv_local, HEAD_WIDTH)[slot_of_span].reshape(
        total_rows, kv_local, HEAD_WIDTH
    )
    value_global = value_all.reshape(slot_count, span_rows, kv_local, HEAD_WIDTH)[
        slot_of_span
    ].reshape(total_rows, kv_local, HEAD_WIDTH)
    key_pos = jnp.arange(total_rows, dtype=jnp.int32)
    key_doc = doc_number(key_pos, doc_starts)
    my_index = lax.axis_index("ctx")
    my_spans = lax.dynamic_slice_in_dim(span_map, 2 * my_index, 2, 0)
    query_all = query_local.reshape(tok_rows, kv_local, query_group_count, HEAD_WIDTH)
    grad_all = grad_local.reshape(tok_rows, kv_local, query_group_count, HEAD_WIDTH)
    span_list = []
    for span_slot in range(2):
        span_id = my_spans[span_slot]
        query_pos = span_id * span_rows + jnp.arange(span_rows, dtype=jnp.int32)
        query_doc = doc_number(query_pos, doc_starts)
        doc_begin = jnp.max(jnp.where(doc_starts <= query_pos[0], doc_starts, 0))
        first_block = doc_begin // block_rows
        last_block = query_pos[span_rows - 1] // block_rows + 1
        query_rows = query_all[span_slot * span_rows : (span_slot + 1) * span_rows]
        grad_rows = grad_all[span_slot * span_rows : (span_slot + 1) * span_rows]
        log_total, row_delta = span_stats(
            query_rows,
            grad_rows,
            query_pos,
            query_doc,
            key_global,
            value_global,
            key_pos,
            key_doc,
            first_block,
            last_block,
            block_rows,
            softmax_scale,
        )
        span_list.append(
            (
                query_rows,
                grad_rows,
                query_pos,
                query_doc,
                first_block,
                last_block,
                log_total,
                row_delta,
            )
        )
    query_parts = []
    key_gradient_sum = jnp.zeros((total_rows, kv_local, HEAD_WIDTH), jnp.float32)
    value_gradient_sum = jnp.zeros((total_rows, kv_local, HEAD_WIDTH), jnp.float32)
    for span_data in span_list:

        def body_block_step(block_id, carry):
            query_acc, key_acc, value_acc = carry
            block_begin = block_id * block_rows
            key_block = lax.dynamic_slice_in_dim(key_global, block_begin, block_rows, 0)
            value_block = lax.dynamic_slice_in_dim(value_global, block_begin, block_rows, 0)
            block_pos = lax.dynamic_slice_in_dim(key_pos, block_begin, block_rows, 0)
            block_doc = lax.dynamic_slice_in_dim(key_doc, block_begin, block_rows, 0)
            weights_b, dscores_b = tile_grads(
                span_data, key_block, value_block, block_pos, block_doc, softmax_scale
            )
            query_acc = query_acc + jnp.einsum(
                "tgjk,kgd->tgjd", dscores_b, key_block, preferred_element_type=jnp.float32
            )
            key_part = jnp.einsum(
                "tgjk,tgjd->kgd", dscores_b, span_data[0], preferred_element_type=jnp.float32
            )
            value_part = jnp.einsum(
                "tgjk,tgjd->kgd", weights_b, span_data[1], preferred_element_type=jnp.float32
            )
            key_acc = lax.dynamic_update_slice_in_dim(
                key_acc,
                lax.dynamic_slice_in_dim(key_acc, block_begin, block_rows, 0) + key_part,
                block_begin,
                0,
            )
            value_acc = lax.dynamic_update_slice_in_dim(
                value_acc,
                lax.dynamic_slice_in_dim(value_acc, block_begin, block_rows, 0) + value_part,
                block_begin,
                0,
            )
            return (query_acc, key_acc, value_acc)

        query_zero = jnp.zeros(span_data[0].shape, jnp.float32)
        query_acc, key_gradient_sum, value_gradient_sum = lax.fori_loop(
            span_data[4],
            span_data[5],
            body_block_step,
            (query_zero, key_gradient_sum, value_gradient_sum),
        )
        query_parts.append(query_acc * softmax_scale)
    key_out = (
        (key_gradient_sum * softmax_scale)
        .reshape(slot_count, span_rows, kv_local * HEAD_WIDTH)[span_map]
        .reshape(total_rows, kv_local * HEAD_WIDTH)
    )
    value_out = value_gradient_sum.reshape(slot_count, span_rows, kv_local * HEAD_WIDTH)[
        span_map
    ].reshape(total_rows, kv_local * HEAD_WIDTH)
    key_grad_local, value_grad_local = (
        lax.psum_scatter(key_out, "ctx", scatter_dimension=0, tiled=True),
        lax.psum_scatter(value_out, "ctx", scatter_dimension=0, tiled=True),
    )
    query_grad = (
        jnp.concatenate(query_parts, axis=0)
        .reshape(tok_rows, kv_local * query_group_count * HEAD_WIDTH)
        .astype(jnp.bfloat16)
    )
    return (
        lax.all_to_all(query_grad, "tp", split_axis=0, concat_axis=1, tiled=True),
        lax.all_to_all(
            key_grad_local.astype(jnp.bfloat16), "tp", split_axis=0, concat_axis=1, tiled=True
        ),
        lax.all_to_all(
            value_grad_local.astype(jnp.bfloat16), "tp", split_axis=0, concat_axis=1, tiled=True
        ),
    )


def solution(mesh):
    in_specs = (
        P(("ctx", "tp"), None),
        P(("ctx", "tp"), None),
        P(("ctx", "tp"), None),
        P(("ctx", "tp"), None),
        P(),
        P(),
    )
    out_specs = (P(("ctx", "tp"), None), P(("ctx", "tp"), None), P(("ctx", "tp"), None))
    return jax.shard_map(shards, mesh=mesh, in_specs=in_specs, out_specs=out_specs, check_vma=False)
```

profile of v0, /device:TPU:8, one launch (start us, length us, event | category | flops | bytes accessed | tf_op | source)
XLA Modules:
  0.0 1197.2 jit_solution(10676968976122791929)
XLA Ops:
  7.2 0.9 copy.117
  8.1 7.5 all_to_all.124
  15.7 0.8 copy.118
  16.5 7.2 all_to_all.125
  23.7 1.9 copy.115
  25.7 5.3 all-to-all-start.3
  34.2 2.0 fusion.66
  46.2 0.8 copy.116
  47.2 3.5 all-to-all-start.1
  50.9 7.0 all-to-all-done.1
  58.3 87.1 %all-gather.5.cloned.1.call-done = bf16[8192,256]{1,0:T(8,128)(2,1)} async-done(((bf16[128,256]{1,0:T(8,128)(2,1)}), bf16[8192,256]{1,0:T(8,128)(2,1)}) %all-gather.5.cloned.1.call-update) | async-done | bytes 4194320 | tf_op jit(solution)/shard_map/all_gather | solution.py:24
  145.4 6.9 reshape.285
  152.4 5.4 copy.71
  157.8 5.3 gather_fusion.1
  163.1 5.3 copy.72
  168.4 105.0 %all-gather.3.cloned.1.call-done = bf16[8192,256]{1,0:T(8,128)(2,1)} async-done(((bf16[128,256]{1,0:T(8,128)(2,1)}), bf16[8192,256]{1,0:T(8,128)(2,1)}) %all-gather.3.cloned.1.call-update) | async-done | bytes 4194320 | tf_op jit(solution)/shard_map/all_gather | solution.py:23
  273.4 6.9 reshape.283
  280.3 5.4 copy.67
  285.7 5.2 gather_fusion
  290.9 5.3 copy.68
  296.3 4.3 while.62
  296.6 1.5 fusion.158
  298.8 1.8 fusion.159
  300.7 8.8 while.60
  301.0 1.5 fusion.137
  303.2 1.8 fusion.138
  305.3 1.5 fusion.137
  307.5 1.8 fusion.138
  309.5 3.8 broadcast.200
  313.3 3.8 broadcast.200.clone
  317.1 18.9 %while.61 = (s32[]{:T(128)}, f32[64,2,8,128]{3,0,2,1:T(8,128)S(1)}, f32[8192,2,128]{2,0,1:T(8,128)}, f32[8192,2,128]{2,0,1:T(8,128)}, s32[]{:T(128)}, /*index=5*...) while((s32[]{:T(128)}, f32[64,2,8,128]{3,0,2,1:T(8,128)S(1)}, ...), condition=%wide.region_10.11_spmd.clone, body=%wide.region_9.10_spmd.clone.sunk | while | flops 675250240 | bytes 14504955 | solution.py:208
  317.4 1.5 fusion.150
  318.9 1.4 fusion.151
  320.3 2.4 fusion.153
  322.7 2.4 fusion.154
  325.1 1.5 fusion.152
  326.8 1.5 fusion.150
  328.4 1.4 fusion.151
  329.8 2.4 fusion.153
  332.2 2.4 fusion.154
  334.5 1.5 fusion.152
  336.1 9.7 while.63
  336.4 1.5 fusion.171
  337.9 1.4 fusion.172
  339.3 2.4 fusion.174
  341.7 2.4 fusion.175
  344.1 1.5 fusion.173
  345.8 4.1 broadcast_multiply_fusion
  349.9 31.3 %copy.84 = f32[8192,2,128]{2,1,0:T(2,128)} copy(f32[8192,2,128]{2,0,1:T(8,128)S(1)} %broadcast_multiply_fusion) | data formatting | bytes 16777216 | tf_op jit(solution)/shard_map/mul | solution.py:216
  381.2 11.5 reshape.287
  392.7 7.7 gather_fusion.2
  400.4 15.4 %copy.86 = f32[8192,2,128]{2,1,0:T(2,128)} copy(f32[8192,2,128]{2,0,1:T(8,128)} %get-tuple-element.314) | data formatting | bytes 16777216 | tf_op jit(solution)/shard_map/while | solution.py:208
  415.8 11.5 reshape.289
  427.3 7.7 gather_fusion.3
  435.6 1.0 convert_element_type.35
  436.6 4.9 all-to-all-start.4
  441.4 363.1 %reduce-scatter.3.cloned.1.call-done = f32[128,256]{1,0:T(8,128)} async-done(((f32[8192,256]{1,0:T(8,128)}), f32[128,256]{1,0:T(8,128)}) %reduce-scatter.3.cloned.1.call-update) | async-done | bytes 131088 | tf_op jit(solution)/shard_map/reduce_scatter | solution.py:224
  804.5 1.5 convert_element_type.36
  806.1 5.8 all-to-all-start.5
  811.8 369.5 %reduce-scatter.5.cloned.1.call-done = f32[128,256]{1,0:T(8,128)} async-done(((f32[8192,256]{1,0:T(8,128)}), f32[128,256]{1,0:T(8,128)}) %reduce-scatter.5.cloned.1.call-update) | async-done | bytes 131088 | tf_op jit(solution)/shard_map/reduce_scatter | solution.py:225
  1181.3 1.5 convert_element_type.37
  1182.9 4.9 all-to-all-start.6
  1187.8 0.8 copy.104
  1189.3 0.8 all-to-all-done.6
  (98 shorter events, 8.5 us)
Async XLA Ops:
  7.2 23.8 %copy-start.2 = (s32[128]{0:T(128)S(1)}, s32[128]{0:T(128)}, u32[]{:S(2)}) copy-start(s32[128]{0:T(128)} %param.19) | copy-start | bytes 1540
  7.2 27.1 %copy-start.1 = (s32[16]{0:T(128)S(1)}, s32[16]{0:T(128)}, u32[]{:S(2)}) copy-start(s32[16]{0:T(128)} %param.18) | copy-start | bytes 196
  7.2 39.0 %copy-start = (bf16[32,8192]{1,0:T(8,128)(2,1)S(1)}, bf16[32,8192]{1,0:T(8,128)(2,1)}, u32[]{:S(2)}) copy-start(bf16[32,8192]{1,0:T(8,128)(2,1)} %param.14) | copy-start | bytes 1572868
  7.2 138.2 %all-gather.5.cloned.1.call-start = ((), (), s32[]{:S(2)}) async-start(), calls=%async_computation.10 | async-start | bytes 4259840 | tf_op jit(solution)/shard_map/all_gather | solution.py:24
  15.6 257.7 %all-gather.3.cloned.1.call-start = ((), (), s32[]{:S(2)}) async-start(), calls=%async_computation.9 | async-start | bytes 4259840 | tf_op jit(solution)/shard_map/all_gather | solution.py:23
  25.7 21.6 %all-to-all-start.3 = ((bf16[32,4,2048]{2,0,1:T(8,128)(2,1)}), bf16[32,4,2048]{2,0,1:T(8,128)(2,1)S(1)}, u32[]{:S(2)}, u32[]{:S(2)}) async-start(bf16[32,4,2048]{2,0,1:T(8,128)(2,1)} %bitcast.223), calls=%async_computation.3 | async-start | bytes 1048576 | tf_op jit(solution)/shard_map/all_to_all | solution.py:104
  47.2 10.7 all-to-all-start.1
  50.7 753.8 %reduce-scatter.3.cloned.1.call-start = ((), (), s32[]{:S(2)}) async-start(), calls=%async_computation.11 | async-start | bytes 8519680 | tf_op jit(solution)/shard_map/reduce_scatter | solution.py:224
  400.4 781.0 %reduce-scatter.5.cloned.1.call-start = ((), (), s32[]{:S(2)}) async-start(), calls=%async_computation.12 | async-start | bytes 8519680 | tf_op jit(solution)/shard_map/reduce_scatter | solution.py:225
  436.6 369.5 %all-to-all-start.4 = ((bf16[4,32,2048]{2,1,0:T(8,128)(2,1)}), bf16[4,32,2048]{2,1,0:T(8,128)(2,1)S(1)}, u32[]{:S(2)}, u32[]{:S(2)}) async-start(bf16[4,32,2048]{2,1,0:T(8,128)(2,1)} %convert_element_type.35), calls=%async_computation.4 | async-start | bytes 1048576 | tf_op jit(solution)/shard_map/all_to_all | solution.py:233
  806.1 376.8 %all-to-all-start.5 = ((bf16[4,32,256]{2,1,0:T(8,128)(2,1)}), bf16[4,32,256]{2,1,0:T(8,128)(2,1)S(1)}, u32[]{:S(2)}, u32[]{:S(2)}) async-start(bf16[4,32,256]{2,1,0:T(8,128)(2,1)} %bitcast.18), calls=%async_computation.6 | async-start | bytes 131072 | tf_op jit(solution)/shard_map/all_to_all | solution.py:234
  1182.9 7.2 all-to-all-start.6
Sparse Core Ops, SparseCore 0:
  15.8 129.6 all-gather.4
  149.0 124.2 all-gather.2
  400.5 403.9 reduce-scatter.2
  806.9 374.3 reduce-scatter.4
where the time goes:
time: 1200 us
  waiting for transfers between devices  933 us (78%)
  local copies, waits for them, and re-layouts  150 us (12%)
  matrix products  37.2 us (3%)
  between operations  25.3 us (2%)
  starting transfers between devices  24.5 us (2%)
  blocking collectives  14.6 us (1%)
  other arithmetic  12.5 us (1%)
    reduce_scatter x1, waiting for transfers between devices, shards(): lax.psum_scatter(value_out, 'ctx', scatter_dimension=0, tiled=True)  370 us
    reduce_scatter x1, waiting for transfers between devices, shards(): lax.psum_scatter(key_out, 'ctx', scatter_dimension=0, tiled=True)  363 us
    all_gather x1, waiting for transfers between devices, fetch_keys(): lax.all_gather(key_local, 'ctx', axis=0, tiled=True)  105 us
    all_gather x1, waiting for transfers between devices, fetch_keys(): lax.all_gather(value_local, 'ctx', axis=0, tiled=True)  87.1 us
    mul x1, local copies, waits for them, and re-layouts, shards(): key_gradient_sum * softmax_scale  31.3 us
  transfers between devices with their start and end apart: 9, of which 6 were waited for; matrix products, arithmetic and copies ran while one was open for 6% of the time, Pallas kernels for 0%

commit v1 on v0

v1 whole, which is shorter than its diff:
```python
import math

import jax
import jax.numpy as jnp
from jax import lax
from jax.experimental import pallas as pl
from jax.experimental.pallas import tpu as pltpu
from jax.sharding import PartitionSpec as P

MESH = pl.DeviceIdType.MESH
HEADS = 8
WIDTH = 128
ROWS = 32
PEERS = 8
RING = 8
SPAN = 64
KEYS = 4096
BLOCK = 256
STRETCH = 2048
SCALE = 1.0 / math.sqrt(WIDTH)
SCALE_LOG2 = SCALE * math.log2(math.e)
NEG_BIG = -1e30


def place():
    c, t = lax.axis_index("ctx"), lax.axis_index("tp")
    return c // PEERS, c % PEERS, t, t // 2, t % 2


def peer_of(p, d):
    return ((p // 4 + d // 4) % 2) * 4 + (p % 4 + d % 4) % 4


def greet(z, p, t, right, left, sibling):
    barrier = pltpu.get_barrier_semaphore()
    targets = [(z * PEERS + peer_of(p, d), t) for d in range(1, PEERS)]
    targets += [(right, t), (left, t), (z * PEERS + p, sibling)]
    for target in targets:
        pl.semaphore_signal(barrier, inc=1, device_id=target, device_id_type=MESH)
    pl.semaphore_wait(barrier, len(targets))


def remote(src, dst, send, recv, target):
    copy = pltpu.make_async_remote_copy(
        src_ref=src, dst_ref=dst, send_sem=send, recv_sem=recv, device_id=target, device_id_type=MESH
    )
    copy.start()
    return copy


def gather_kernel(
    q, do, k, v, qg, dog, kv, kv_s, kv_r, q_s, q_r, ring_s, ring_r, sib_s, sib_r
):
    z, p, t, y_lo, core = place()
    right, left = ((z + 1) % RING) * PEERS + p, ((z + RING - 1) % RING) * PEERS + p
    here = z * PEERS + p
    sibling = y_lo * 2 + 1 - core
    greet(z, p, t, right, left, sibling)
    small, large, ring, across = [], [], {}, []
    for d in range(1, PEERS):
        other = peer_of(p, d)
        for part, src in enumerate((k, v)):
            small.append(
                remote(
                    src.at[:, pl.ds(pl.multiple_of(other * WIDTH, WIDTH), WIDTH)],
                    kv.at[core, z, part, pl.ds(p * ROWS, ROWS)],
                    kv_s.at[d, part],
                    kv_r.at[d, part],
                    (z * PEERS + other, t),
                )
            )
    own = []
    for part, src in enumerate((k, v)):
        copy = pltpu.make_async_copy(
            src.at[:, pl.ds(pl.multiple_of(p * WIDTH, WIDTH), WIDTH)],
            kv.at[core, z, part, pl.ds(p * ROWS, ROWS)],
            kv_s.at[0, part],
        )
        copy.start()
        own.append(copy)
    wide = HEADS * WIDTH
    for d in range(1, PEERS):
        other = peer_of(p, d)
        for part, (src, dst) in enumerate(((q, qg), (do, dog))):
            large.append(
                remote(
                    src.at[:, pl.ds(pl.multiple_of(other * wide, wide), wide)],
                    dst.at[p],
                    q_s.at[d, part],
                    q_r.at[d, part],
                    (z * PEERS + other, t),
                )
            )
    own_large = []
    for part, (src, dst) in enumerate(((q, qg), (do, dog))):
        copy = pltpu.make_async_copy(
            src.at[:, pl.ds(pl.multiple_of(p * wide, wide), wide)], dst.at[p], q_s.at[0, part]
        )
        copy.start()
        own_large.append(copy)
    for copy in own:
        copy.wait()
    for copy in small:
        copy.wait_recv()

    def forward(step, way, part, offset):
        chunk = kv.at[core, (z + offset) % RING, part]
        target = (right if way == 0 else left, t)
        ring[step, way, part] = remote(
            chunk, chunk, ring_s.at[step, way, part], ring_r.at[step, way, part], target
        )

    def share(part, offset):
        chunk = kv.at[core, (z + offset) % RING, part]
        across.append(
            remote(chunk, chunk, sib_s.at[offset, part], sib_r.at[offset, part], (here, sibling))
        )

    for part in range(2):
        for way in range(2):
            forward(0, way, part, 0)
    for part in range(2):
        share(part, 0)
    for step in range(1, 5):
        for part in range(2):
            for way in range(2):
                if step == 4 and way != part:
                    continue
                offset = RING - step if way == 0 else step
                ring[step - 1, way, part].wait_recv()
                if step < 3 or (step == 3 and way == part):
                    forward(step, way, part, offset)
                share(part, offset)
    for copy in across:
        copy.wait_recv()
    for copy in large:
        copy.wait()
    for copy in own_large:
        copy.wait()
    for copy in small + list(ring.values()) + across:
        copy.wait_send()


def attention_kernel(
    spans, starts, q, do, kv, dq, dkv, key, value, key_t, dkey, dvalue, scores, dweights, dq_t
):
    z, p, t, y_lo, core = place()
    del p, t
    base = y_lo * KEYS

    def local_row(c, half):
        return pl.multiple_of(spans[2 * c + y_lo] * SPAN - base + half * ROWS, ROWS)

    def place_keys(i, _):
        for half in range(2):
            row = local_row(i, half)
            slot = pl.multiple_of((i % PEERS) * ROWS, ROWS)
            key[pl.ds(row, ROWS)] = kv[half, i // PEERS, 0, pl.ds(slot, ROWS)]
            value[pl.ds(row, ROWS)] = kv[half, i // PEERS, 1, pl.ds(slot, ROWS)]
        return 0

    lax.fori_loop(0, RING * PEERS, place_keys, 0)

    def turn_keys(b, _):
        rows = pl.ds(pl.multiple_of(b * BLOCK, BLOCK), BLOCK)
        key_t[b] = key[rows].T
        dkey[rows] = jnp.zeros((BLOCK, WIDTH), jnp.float32)
        dvalue[rows] = jnp.zeros((BLOCK, WIDTH), jnp.float32)
        return 0

    lax.fori_loop(0, KEYS // BLOCK, turn_keys, 0)
    columns = HEADS * ROWS

    def tile(i, _):
        first = local_row(z * PEERS + i, core)
        queries = jnp.concatenate(
            [q[i, :, h * WIDTH : (h + 1) * WIDTH] for h in range(HEADS)], axis=0
        )
        grads = jnp.concatenate(
            [do[i, :, h * WIDTH : (h + 1) * WIDTH] for h in range(HEADS)], axis=0
        )
        row = first + lax.broadcasted_iota(jnp.int32, (1, columns), 1) % ROWS
        begin = jnp.int32(0)
        low = jnp.zeros((1, columns), jnp.int32)
        for n in range(starts.shape[0]):
            start = starts[n] - base
            begin = jnp.where(start <= first, jnp.maximum(begin, start), begin)
            low = jnp.where(start <= row, jnp.maximum(low, start), low)
        begin_block = begin // BLOCK
        end_block = (first + ROWS - 1) // BLOCK + 1

        def score_step(b, top):
            rows = pl.ds(pl.multiple_of(b * BLOCK, BLOCK), BLOCK)
            here = pl.ds(pl.multiple_of((b % (STRETCH // BLOCK)) * BLOCK, BLOCK), BLOCK)
            s = lax.dot_general(
                key[rows], queries, (((1,), (1,)), ((), ())), preferred_element_type=jnp.float32
            )
            dweights[here] = lax.dot_general(
                value[rows], grads, (((1,), (1,)), ((), ())), preferred_element_type=jnp.float32
            )
            pos = b * BLOCK + lax.broadcasted_iota(jnp.int32, (BLOCK, columns), 0)
            s = jnp.where((pos >= low) & (pos <= row), s * SCALE_LOG2, NEG_BIG)
            scores[here] = s
            return jnp.maximum(top, jnp.max(s.reshape(BLOCK // 8, 8, columns), axis=0))

        top = lax.fori_loop(
            begin_block, end_block, score_step, jnp.full((8, columns), NEG_BIG, jnp.float32)
        )
        top = jnp.max(top, axis=0, keepdims=True)

        def sum_step(b, carry):
            total, dot = carry
            here = pl.ds(pl.multiple_of((b % (STRETCH // BLOCK)) * BLOCK, BLOCK), BLOCK)
            e = jnp.exp2(scores[here] - top)
            scores[here] = e
            total += jnp.sum(e.reshape(BLOCK // 8, 8, columns), axis=0)
            dot += jnp.sum((e * dweights[here]).reshape(BLOCK // 8, 8, columns), axis=0)
            return total, dot

        zero = jnp.zeros((8, columns), jnp.float32)
        total, dot = lax.fori_loop(begin_block, end_block, sum_step, (zero, zero))
        inverse = 1.0 / jnp.sum(total, axis=0, keepdims=True)
        delta = jnp.sum(dot, axis=0, keepdims=True) * inverse
        dq_t[...] = jnp.zeros_like(dq_t)

        def grad_step(b, _):
            rows = pl.ds(pl.multiple_of(b * BLOCK, BLOCK), BLOCK)
            here = pl.ds(pl.multiple_of((b % (STRETCH // BLOCK)) * BLOCK, BLOCK), BLOCK)
            w = scores[here] * inverse
            ds = (w * (dweights[here] - delta)).astype(jnp.bfloat16)
            dvalue[rows] += jnp.dot(
                w.astype(jnp.bfloat16), grads, preferred_element_type=jnp.float32
            )
            dkey[rows] += jnp.dot(ds, queries, preferred_element_type=jnp.float32)
            dq_t[...] += jnp.dot(key_t[b], ds, preferred_element_type=jnp.float32)
            return 0

        lax.fori_loop(begin_block, end_block, grad_step, 0)
        out = (dq_t[...] * SCALE).T.astype(jnp.bfloat16)
        for h in range(HEADS):
            dq[i, :, h * WIDTH : (h + 1) * WIDTH] = out[h * ROWS : (h + 1) * ROWS]
        return 0

    lax.fori_loop(0, PEERS, tile, 0)

    def give_keys(i, _):
        for half in range(2):
            row = local_row(i, half)
            slot = pl.multiple_of((i % PEERS) * ROWS, ROWS)
            dkv[half, i // PEERS, 0, pl.ds(slot, ROWS)] = (dkey[pl.ds(row, ROWS)] * SCALE).astype(
                jnp.bfloat16
            )
            dkv[half, i // PEERS, 1, pl.ds(slot, ROWS)] = dvalue[pl.ds(row, ROWS)].astype(
                jnp.bfloat16
            )
        return 0

    lax.fori_loop(0, RING * PEERS, give_keys, 0)


def scatter_kernel(
    dqp, dkv, dq, dk, dv, own, pair, got, sent, final,
    own_s, pair_s, pair_r, q_s, q_r, ring_s, ring_r, kv_s, kv_r,
):
    z, p, t, y_lo, core = place()
    right, left = ((z + 1) % RING) * PEERS + p, ((z + RING - 1) % RING) * PEERS + p
    here = z * PEERS + p
    sibling = y_lo * 2 + 1 - core
    order = (4, 3, 5, 2, 6, 1, 7, 0)
    loads, across, large, ring, small = {}, {}, [], {}, []
    for offset in order:
        copy = pltpu.make_async_copy(
            dkv.at[core, (z + offset) % RING], own.at[offset], own_s.at[offset]
        )
        copy.start()
        loads[offset] = copy
    greet(z, p, t, right, left, sibling)
    for offset in order:
        across[offset] = remote(
            dkv.at[1 - core, (z + offset) % RING],
            pair.at[offset],
            pair_s.at[offset],
            pair_r.at[offset],
            (here, sibling),
        )
    wide = HEADS * WIDTH
    columns = pl.ds(pl.multiple_of(p * wide, wide), wide)
    for d in range(1, PEERS):
        other = peer_of(p, d)
        large.append(
            remote(
                dqp.at[other], dq.at[:, columns], q_s.at[d], q_r.at[d], (z * PEERS + other, t)
            )
        )
    own_large = pltpu.make_async_copy(dqp.at[p], dq.at[:, columns], q_s.at[0])
    own_large.start()

    def term(offset, part):
        return own[offset, part].astype(jnp.float32) + pair[offset, part].astype(jnp.float32)

    for step in range(4):
        for way in range(2):
            offset = 4 - step if way == 0 else 4 + step
            if offset in loads:
                loads.pop(offset).wait()
                across[offset].wait_recv()
            for part in range(2):
                if step == 0 and part != way:
                    continue
                value = term(offset, part)
                if step > 1 or (step == 1 and part == way):
                    ring[step - 1, way, part].wait_recv()
                    value += got[step - 1, way, part].astype(jnp.float32)
                sent[step, way, part] = value.astype(jnp.bfloat16)
                ring[step, way, part] = remote(
                    sent.at[step, way, part],
                    got.at[step, way, part],
                    ring_s.at[step, way, part],
                    ring_r.at[step, way, part],
                    (right if way == 0 else left, t),
                )
    loads.pop(0).wait()
    across[0].wait_recv()
    narrow = pl.ds(pl.multiple_of(p * WIDTH, WIDTH), WIDTH)
    own_small = []
    for part, dst in enumerate((dk, dv)):
        value = term(0, part)
        for way in range(2):
            ring[3, way, part].wait_recv()
            value += got[3, way, part].astype(jnp.float32)
        final[part] = value.astype(jnp.bfloat16)
        for d in range(1, PEERS):
            other = peer_of(p, d)
            small.append(
                remote(
                    final.at[part, pl.ds(other * ROWS, ROWS)],
                    dst.at[:, narrow],
                    kv_s.at[d, part],
                    kv_r.at[d, part],
                    (z * PEERS + other, t),
                )
            )
        copy = pltpu.make_async_copy(
            final.at[part, pl.ds(p * ROWS, ROWS)], dst.at[:, narrow], kv_s.at[0, part]
        )
        copy.start()
        own_small.append(copy)
    for copy in large + small:
        copy.wait()
    for copy in [own_large] + own_small:
        copy.wait()
    for copy in list(ring.values()) + list(across.values()):
        copy.wait_send()


def shards(queries, key_head_states, value_head_states, output_gradient, doc_starts, span_map):
    anywhere = pl.BlockSpec(memory_space=pl.ANY)
    vmem = pl.BlockSpec(memory_space=pltpu.VMEM)
    smem = pl.BlockSpec(memory_space=pltpu.SMEM)
    dma = pltpu.SemaphoreType.DMA
    b16, f32 = jnp.bfloat16, jnp.float32
    wide = HEADS * WIDTH
    rows = PEERS * ROWS
    grouped = jax.ShapeDtypeStruct((PEERS, ROWS, wide), b16)
    chunks = jax.ShapeDtypeStruct((2, RING, 2, rows, WIDTH), b16)
    qg, dog, kv = pl.pallas_call(
        gather_kernel,
        out_shape=(grouped, grouped, chunks),
        in_specs=[anywhere] * 4,
        out_specs=(anywhere,) * 3,
        scratch_shapes=[
            dma((PEERS, 2)),
            dma((PEERS, 2)),
            dma((PEERS, 2)),
            dma((PEERS, 2)),
            dma((4, 2, 2)),
            dma((4, 2, 2)),
            dma((RING, 2)),
            dma((RING, 2)),
        ],
        compiler_params=pltpu.CompilerParams(collective_id=0, has_side_effects=True),
        name="gather_heads",
    )(queries, output_gradient, key_head_states, value_head_states)
    dqp, dkv = pl.pallas_call(
        attention_kernel,
        out_shape=(grouped, chunks),
        in_specs=[smem, smem, vmem, vmem, vmem],
        out_specs=(vmem, vmem),
        scratch_shapes=[
            pltpu.VMEM((KEYS, WIDTH), b16),
            pltpu.VMEM((KEYS, WIDTH), b16),
            pltpu.VMEM((KEYS // BLOCK, WIDTH, BLOCK), b16),
            pltpu.VMEM((KEYS, WIDTH), f32),
            pltpu.VMEM((KEYS, WIDTH), f32),
            pltpu.VMEM((STRETCH, HEADS * ROWS), f32),
            pltpu.VMEM((STRETCH, HEADS * ROWS), f32),
            pltpu.VMEM((WIDTH, HEADS * ROWS), f32),
        ],
        compiler_params=pltpu.CompilerParams(vmem_limit_bytes=48 * 1024 * 1024),
        name="attention_grads",
    )(span_map, doc_starts, qg, dog, kv)
    return pl.pallas_call(
        scatter_kernel,
        out_shape=(
            jax.ShapeDtypeStruct((ROWS, PEERS * wide), b16),
            jax.ShapeDtypeStruct((ROWS, PEERS * WIDTH), b16),
            jax.ShapeDtypeStruct((ROWS, PEERS * WIDTH), b16),
        ),
        in_specs=[anywhere] * 2,
        out_specs=(anywhere,) * 3,
        scratch_shapes=[
            pltpu.VMEM((RING, 2, rows, WIDTH), b16),
            pltpu.VMEM((RING, 2, rows, WIDTH), b16),
            pltpu.VMEM((4, 2, 2, rows, WIDTH), b16),
            pltpu.VMEM((4, 2, 2, rows, WIDTH), b16),
            pltpu.VMEM((2, rows, WIDTH), b16),
            dma((RING,)),
            dma((RING,)),
            dma((RING,)),
            dma((PEERS,)),
            dma((PEERS,)),
            dma((4, 2, 2)),
            dma((4, 2, 2)),
            dma((PEERS, 2)),
            dma((PEERS, 2)),
        ],
        compiler_params=pltpu.CompilerParams(
            collective_id=1, has_side_effects=True, vmem_limit_bytes=32 * 1024 * 1024
        ),
        name="scatter_grads",
    )(dqp, dkv)


def solution(mesh):
    rows = P(("ctx", "tp"), None)
    in_specs = (rows, rows, rows, rows, P(), P())
    return jax.shard_map(
        shards, mesh=mesh, in_specs=in_specs, out_specs=(rows, rows, rows), check_vma=False
    )
```

time: 1200 us -> 95 us (0.08)
  the two profiles are of different devices: /device:TPU:8 before, /device:TPU:16 now
where the time goes in v1:
time: 95 us; the launch traced here: 94.8 us
  Pallas kernels  87.1 us (92%)
  local copies, waits for them, and re-layouts  7.03 us (7%)
    pallas_call x1, Pallas kernels, shards(): pl.pallas_call(gather_kernel, out_shape=(grouped, grouped, chunks), in_sp...  34.3 us
    pallas_call x1, Pallas kernels, shards(): pl.pallas_call(scatter_kernel, out_shape=(jax.ShapeDtypeStruct((ROWS, PEE...  33 us
    pallas_call x1, Pallas kernels, shards(): pl.pallas_call(attention_kernel, out_shape=(grouped, chunks), in_specs=[s...  19.8 us
    unnamed x13, local copies, waits for them, and re-layouts  7.03 us

profile of v1, /device:TPU:16, one launch (start us, length us, event | category | flops | bytes accessed | tf_op | source)
XLA Modules:
  0.0 94.8 jit_solution(1989957033280305103)
XLA Ops:
  0.6 34.3 %gather_heads.1 = (bf16[8,32,1024]{2,1,0:T(8,128)(2,1)}, bf16[8,32,1024]{2,1,0:T(8,128)(2,1)}, bf16[2,8,2,256,128]{4,3,2,1,0:T(8,128)(2,1)}) custom-call(bf16[32,8192]{1,0:T(8,128)(2,1)} %q.1, bf16[32,8192]{1,0:T(8,128)(2,1)} %do.1, bf16[32,1024]{1,0:T(8,128)(2,1)} %k.1, bf16[32,1024]{1,0:T(8,128)(2,1)} %v.1), custom_call_target="tpu_custom_call" | custom-call | tf_op jit(solution)/shard_map/gather_heads/pallas_call | solution.py:366
  34.9 0.0 copy-start
  34.9 1.6 %copy-done = bf16[2,8,2,256,128]{4,3,2,1,0:T(8,128)(2,1)S(1)} copy-done((bf16[2,8,2,256,128]{4,3,2,1,0:T(8,128)(2,1)S(1)}, bf16[2,8,2,256,128]{4,3,2,1,0:T(8,128)(2,1)}, u32[]{:S(2)}) %copy-start) | copy-done | bytes 2097176
  36.5 0.0 copy-start.1
  36.5 1.0 %copy-done.1 = bf16[8,32,1024]{2,1,0:T(8,128)(2,1)S(1)} copy-done((bf16[8,32,1024]{2,1,0:T(8,128)(2,1)S(1)}, bf16[8,32,1024]{2,1,0:T(8,128)(2,1)}, u32[]{:S(2)}) %copy-start.1) | copy-done | bytes 524312
  37.5 0.0 copy-start.2
  37.5 1.0 %copy-done.2 = bf16[8,32,1024]{2,1,0:T(8,128)(2,1)S(1)} copy-done((bf16[8,32,1024]{2,1,0:T(8,128)(2,1)S(1)}, bf16[8,32,1024]{2,1,0:T(8,128)(2,1)}, u32[]{:S(2)}) %copy-start.2) | copy-done | bytes 524312
  38.6 0.0 copy-start.3
  38.6 0.7 copy-done.3
  39.2 0.0 copy-start.4
  39.2 0.7 copy-done.4
  39.9 19.8 %attention_grads.1 = (bf16[8,32,1024]{2,1,0:T(8,128)(2,1)S(1)}, bf16[2,8,2,256,128]{4,3,2,1,0:T(8,128)(2,1)S(1)}) custom-call(s32[128]{0:T(128)S(1)} %copy-done.3, s32[16]{0:T(128)S(1)} %copy-done.4, bf16[8,32,1024]{2,1,0:T(8,128)(2,1)S(1)} %copy-done.1, bf16[8,32,1024]{2,1,0:T(8,128)(2,1)S(1)} %copy-done.2, bf16[2,8,2,256,128]{4,3,2,1,0:T(8,128)(2,1)S(1)} %copy-done), custom_call_target="tpu_custom_call" | custom-call | tf_op jit(solution)/shard_map/attention_grads/pallas_call | solution.py:384
  59.7 33.0 %scatter_grads.1 = (bf16[32,8192]{1,0:T(8,128)(2,1)S(1)}, bf16[32,1024]{1,0:T(8,128)(2,1)S(1)}, bf16[32,1024]{1,0:T(8,128)(2,1)S(1)}) custom-call(bf16[8,32,1024]{2,1,0:T(8,128)(2,1)S(1)} %get-tuple-element.11.dqp, bf16[2,8,2,256,128]{4,3,2,1,0:T(8,128)(2,1)S(1)} %get-tuple-element.12.dkv), custom_call_target="tpu_custom_call" | custom-call | tf_op jit(solution)/shard_map/scatter_grads/pallas_call | solution.py:402
  92.7 0.8 copy.12
  93.5 0.6 copy.13
  94.2 0.6 copy.14
Async XLA Ops:
  34.9 1.6 %copy-start = (bf16[2,8,2,256,128]{4,3,2,1,0:T(8,128)(2,1)S(1)}, bf16[2,8,2,256,128]{4,3,2,1,0:T(8,128)(2,1)}, u32[]{:S(2)}) copy-start(bf16[2,8,2,256,128]{4,3,2,1,0:T(8,128)(2,1)} %get-tuple-element.10.kv) | copy-start | bytes 6291460
  36.5 1.0 %copy-start.1 = (bf16[8,32,1024]{2,1,0:T(8,128)(2,1)S(1)}, bf16[8,32,1024]{2,1,0:T(8,128)(2,1)}, u32[]{:S(2)}) copy-start(bf16[8,32,1024]{2,1,0:T(8,128)(2,1)} %get-tuple-element.8.q) | copy-start | bytes 1572868
  37.5 1.0 %copy-start.2 = (bf16[8,32,1024]{2,1,0:T(8,128)(2,1)S(1)}, bf16[8,32,1024]{2,1,0:T(8,128)(2,1)}, u32[]{:S(2)}) copy-start(bf16[8,32,1024]{2,1,0:T(8,128)(2,1)} %get-tuple-element.9.do) | copy-start | bytes 1572868
  38.6 0.7 copy-start.3
  39.2 0.7 copy-start.4

commit v2 on v1

v2 whole, which is shorter than its diff:
```python
import math

import jax
import jax.numpy as jnp
from jax import lax
from jax.experimental import pallas as pl
from jax.experimental.pallas import tpu as pltpu
from jax.sharding import PartitionSpec as P

MESH = pl.DeviceIdType.MESH
ORDER = (1, 3, 2, 4, 5, 7, 6)
HEADS = 8
WIDTH = 128
ROWS = 32
PEERS = 8
RING = 8
SPAN = 64
KEYS = 4096
BLOCK = 512
STRETCH = 2048
SCALE = 1.0 / math.sqrt(WIDTH)
SCALE_LOG2 = SCALE * math.log2(math.e)
NEG_BIG = -1e30


def place():
    c, t = lax.axis_index("ctx"), lax.axis_index("tp")
    return c // PEERS, c % PEERS, t, t // 2, t % 2


def peer_of(p, d):
    return ((p // 4 + d // 4) % 2) * 4 + (p % 4 + d % 4) % 4


def half_rows(p, half):
    rows = PEERS * ROWS // 2
    return pl.ds(pl.multiple_of(((p // 4 + half) % 2) * rows, rows), rows)


def greet(z, p, t, right, left, sibling):
    barrier = pltpu.get_barrier_semaphore()
    targets = [(z * PEERS + peer_of(p, d), t) for d in range(1, PEERS)]
    targets += [(right, t), (left, t), (z * PEERS + p, sibling)]
    for target in targets:
        pl.semaphore_signal(barrier, inc=1, device_id=target, device_id_type=MESH)
    pl.semaphore_wait(barrier, len(targets))


def remote(src, dst, send, recv, target):
    copy = pltpu.make_async_remote_copy(
        src_ref=src, dst_ref=dst, send_sem=send, recv_sem=recv, device_id=target, device_id_type=MESH
    )
    copy.start()
    return copy


def gather_kernel(
    q, do, k, v, qg, dog, kv, kv_s, kv_r, q_s, q_r, ring_s, ring_r, sib_s, sib_r
):
    z, p, t, y_lo, core = place()
    right, left = ((z + 1) % RING) * PEERS + p, ((z + RING - 1) % RING) * PEERS + p
    here = z * PEERS + p
    sibling = y_lo * 2 + 1 - core
    greet(z, p, t, right, left, sibling)
    small, large, ring, across, own = {}, [], {}, [], []
    for part, src in enumerate((k, v)):
        copy = pltpu.make_async_copy(
            src.at[:, pl.ds(pl.multiple_of(p * WIDTH, WIDTH), WIDTH)],
            kv.at[core, z, part, pl.ds(p * ROWS, ROWS)],
            kv_s.at[0, part],
        )
        copy.start()
        own.append(copy)
    for d in ORDER:
        other = peer_of(p, d)
        for part, src in enumerate((k, v)):
            small[d, part] = remote(
                src.at[:, pl.ds(pl.multiple_of(other * WIDTH, WIDTH), WIDTH)],
                kv.at[core, z, part, pl.ds(p * ROWS, ROWS)],
                kv_s.at[d, part],
                kv_r.at[d, part],
                (z * PEERS + other, t),
            )
    wide = HEADS * WIDTH
    for d in ORDER:
        other = peer_of(p, d)
        for part, (src, dst) in enumerate(((q, qg), (do, dog))):
            large.append(
                remote(
                    src.at[:, pl.ds(pl.multiple_of(other * wide, wide), wide)],
                    dst.at[p],
                    q_s.at[d, part],
                    q_r.at[d, part],
                    (z * PEERS + other, t),
                )
            )
    own_large = []
    for part, (src, dst) in enumerate(((q, qg), (do, dog))):
        copy = pltpu.make_async_copy(
            src.at[:, pl.ds(pl.multiple_of(p * wide, wide), wide)], dst.at[p], q_s.at[0, part]
        )
        copy.start()
        own_large.append(copy)

    def piece(part, half, offset):
        return kv.at[core, (z + offset) % RING, part, half_rows(p, half)]

    def forward(step, way, part, half, offset):
        chunk = piece(part, half, offset)
        key = step, way, part, half
        target = (right if way == 0 else left, t)
        ring[key] = remote(chunk, chunk, ring_s.at[key], ring_r.at[key], target)

    def share(part, half, offset):
        chunk = piece(part, half, offset)
        key = offset, part, half
        across.append(remote(chunk, chunk, sib_s.at[key], sib_r.at[key], (here, sibling)))

    for half in range(2):
        for part in range(2):
            if half == 0:
                own[part].wait()
            for d in ORDER:
                if d // 4 == half:
                    small[d, part].wait_recv()
            for way in range(2):
                forward(0, way, part, half, 0)
            share(part, half, 0)
    for step in range(1, 5):
        for half in range(2):
            for part in range(2):
                for way in range(2):
                    if step == 4 and way != part:
                        continue
                    offset = RING - step if way == 0 else step
                    ring[step - 1, way, part, half].wait_recv()
                    if step < 3 or (step == 3 and way == part):
                        forward(step, way, part, half, offset)
                    share(part, half, offset)
    for copy in across:
        copy.wait_recv()
    for copy in large:
        copy.wait()
    for copy in own_large:
        copy.wait()
    for copy in list(small.values()) + list(ring.values()) + across:
        copy.wait_send()


def attention_kernel(
    spans_in, starts_in, q, do, kv, dq, dkv,
    spans, starts, key, value, key_t, dkey, dvalue, powers, dweights, tops, dq_t, sems,
):
    loads = [
        pltpu.make_async_copy(spans_in, spans, sems.at[0]),
        pltpu.make_async_copy(starts_in, starts, sems.at[1]),
    ]
    for copy in loads:
        copy.start()
    z, p, t, y_lo, core = place()
    del p, t
    base = y_lo * KEYS

    def clear(b, _):
        rows = pl.ds(pl.multiple_of(b * BLOCK, BLOCK), BLOCK)
        dkey[rows] = jnp.zeros((BLOCK, WIDTH), jnp.float32)
        dvalue[rows] = jnp.zeros((BLOCK, WIDTH), jnp.float32)
        return 0

    lax.fori_loop(0, KEYS // BLOCK, clear, 0)
    value[KEYS:] = jnp.zeros((BLOCK, WIDTH), jnp.bfloat16)
    key[KEYS:] = jnp.zeros((BLOCK, WIDTH), jnp.bfloat16)
    key_t[:, KEYS:] = jnp.zeros((WIDTH, BLOCK), jnp.bfloat16)
    for copy in loads:
        copy.wait()

    def local_row(c, half):
        return pl.multiple_of(spans[2 * c + y_lo] * SPAN - base + half * ROWS, ROWS)

    def place_keys(i, _):
        for j in range(PEERS):
            for half in range(2):
                row = local_row(i * PEERS + j, half)
                key[pl.ds(row, ROWS)] = kv[half, i, 0, j * ROWS : (j + 1) * ROWS]
                value[pl.ds(row, ROWS)] = kv[half, i, 1, j * ROWS : (j + 1) * ROWS]
        return 0

    lax.fori_loop(0, RING, place_keys, 0)

    def turn_keys(b, _):
        rows = pl.ds(pl.multiple_of(b * BLOCK, BLOCK), BLOCK)
        key_t[:, rows] = key[rows].T
        return 0

    lax.fori_loop(0, KEYS // BLOCK, turn_keys, 0)
    columns = HEADS * ROWS

    def tile(i, _):
        first = local_row(z * PEERS + i, core)
        queries = jnp.concatenate(
            [q[i, :, h * WIDTH : (h + 1) * WIDTH] for h in range(HEADS)], axis=0
        )
        grads = jnp.concatenate(
            [do[i, :, h * WIDTH : (h + 1) * WIDTH] for h in range(HEADS)], axis=0
        )
        row = first + lax.broadcasted_iota(jnp.int32, (1, columns), 1) % ROWS
        begin = jnp.int32(0)
        low = jnp.zeros((1, columns), jnp.int32)
        for n in range(starts.shape[0]):
            start = starts[n] - base
            begin = jnp.where(start <= first, jnp.maximum(begin, start), begin)
            low = jnp.where(start <= row, jnp.maximum(low, start), low)
        begin = (begin // WIDTH) * WIDTH
        steps = (first + ROWS - begin + BLOCK - 1) // BLOCK

        def score_step(b, carry):
            top, total, dot = carry
            here = pl.multiple_of(begin + b * BLOCK, WIDTH)
            rows = pl.ds(here, BLOCK)
            s = lax.dot_general(
                key[rows], queries, (((1,), (1,)), ((), ())), preferred_element_type=jnp.float32
            )
            dw = lax.dot_general(
                value[rows], grads, (((1,), (1,)), ((), ())), preferred_element_type=jnp.float32
            )
            dweights[b] = dw
            pos = here + lax.broadcasted_iota(jnp.int32, (BLOCK, columns), 0)
            s = jnp.where((pos >= low) & (pos <= row), s * SCALE_LOG2, NEG_BIG)
            new = jnp.maximum(top, jnp.max(s, axis=0, keepdims=True))
            e = jnp.exp2(s - new)
            powers[b] = e
            tops[b] = new
            factor = jnp.exp2(top - new)
            total = total * factor + jnp.sum(e, axis=0, keepdims=True)
            dot = dot * factor + jnp.sum(e * dw, axis=0, keepdims=True)
            return new, total, dot

        zero = jnp.zeros((1, columns), jnp.float32)
        top, total, dot = lax.fori_loop(0, steps, score_step, (zero + NEG_BIG, zero, zero))
        inverse = 1.0 / total
        delta = dot * inverse
        dq_t[...] = jnp.zeros_like(dq_t)

        def grad_step(b, _):
            here = pl.multiple_of(begin + b * BLOCK, WIDTH)
            rows = pl.ds(here, BLOCK)
            w = powers[b] * (jnp.exp2(tops[b] - top) * inverse)
            ds = (w * (dweights[b] - delta)).astype(jnp.bfloat16)
            dvalue[rows] += jnp.dot(
                w.astype(jnp.bfloat16), grads, preferred_element_type=jnp.float32
            )
            dkey[rows] += jnp.dot(ds, queries, preferred_element_type=jnp.float32)
            dq_t[...] += jnp.dot(key_t[:, rows], ds, preferred_element_type=jnp.float32)
            return 0

        lax.fori_loop(0, steps, grad_step, 0)
        out = (dq_t[...] * SCALE).T.astype(jnp.bfloat16)
        for h in range(HEADS):
            dq[i, :, h * WIDTH : (h + 1) * WIDTH] = out[h * ROWS : (h + 1) * ROWS]
        return 0

    lax.fori_loop(0, PEERS, tile, 0)

    def give_keys(i, _):
        for j in range(PEERS):
            for half in range(2):
                rows = pl.ds(local_row(i * PEERS + j, half), ROWS)
                slot = slice(j * ROWS, (j + 1) * ROWS)
                dkv[half, i, 0, slot] = (dkey[rows] * SCALE).astype(jnp.bfloat16)
                dkv[half, i, 1, slot] = dvalue[rows].astype(jnp.bfloat16)
        return 0

    lax.fori_loop(0, RING, give_keys, 0)


def scatter_kernel(
    dqp, dkv, dq, dk, dv, pair, got, sent, final,
    pair_s, pair_r, q_s, q_r, ring_s, ring_r, kv_s, kv_r,
):
    z, p, t, y_lo, core = place()
    right, left = ((z + 1) % RING) * PEERS + p, ((z + RING - 1) % RING) * PEERS + p
    here = z * PEERS + p
    sibling = y_lo * 2 + 1 - core
    across, large, ring, small = {}, [], {}, []
    greet(z, p, t, right, left, sibling)
    for offset in (4, 3, 5, 2, 6, 1, 7, 0):
        across[offset] = remote(
            dkv.at[1 - core, (z + offset) % RING],
            pair.at[offset],
            pair_s.at[offset],
            pair_r.at[offset],
            (here, sibling),
        )
    wide = HEADS * WIDTH
    columns = pl.ds(pl.multiple_of(p * wide, wide), wide)
    for d in ORDER:
        other = peer_of(p, d)
        large.append(
            remote(
                dqp.at[other], dq.at[:, columns], q_s.at[d], q_r.at[d], (z * PEERS + other, t)
            )
        )
    own_large = pltpu.make_async_copy(dqp.at[p], dq.at[:, columns], q_s.at[0])
    own_large.start()
    met = set()

    def term(offset, part, half):
        if offset not in met:
            across[offset].wait_recv()
            met.add(offset)
        rows = half_rows(p, half)
        mine = dkv[core, (z + offset) % RING, part, rows].astype(jnp.float32)
        return mine + pair[offset, part, rows].astype(jnp.float32)

    def arrived(step, way, part, half):
        ring[step, way, part, half].wait_recv()
        return got[step, way, part, half_rows(p, half)].astype(jnp.float32)

    for step in range(4):
        for half in (1, 0):
            for part in range(2):
                for way in range(2):
                    if step == 0 and part != way:
                        continue
                    value = term(4 - step if way == 0 else 4 + step, part, half)
                    if step > 1 or (step == 1 and part == way):
                        value += arrived(step - 1, way, part, half)
                    rows = half_rows(p, half)
                    key = step, way, part, half
                    sent[step, way, part, rows] = value.astype(jnp.bfloat16)
                    ring[key] = remote(
                        sent.at[step, way, part, rows],
                        got.at[step, way, part, rows],
                        ring_s.at[key],
                        ring_r.at[key],
                        (right if way == 0 else left, t),
                    )
    narrow = pl.ds(pl.multiple_of(p * WIDTH, WIDTH), WIDTH)
    own_small = []
    for half in (1, 0):
        for part, dst in enumerate((dk, dv)):
            value = term(0, part, half)
            for way in range(2):
                value += arrived(3, way, part, half)
            final[part, half_rows(p, half)] = value.astype(jnp.bfloat16)
            for d in range(PEERS):
                if d // 4 != half:
                    continue
                other = peer_of(p, d)
                src = final.at[part, pl.ds(other * ROWS, ROWS)]
                if d == 0:
                    copy = pltpu.make_async_copy(src, dst.at[:, narrow], kv_s.at[0, part])
                    copy.start()
                    own_small.append(copy)
                else:
                    small.append(
                        remote(
                            src,
                            dst.at[:, narrow],
                            kv_s.at[d, part],
                            kv_r.at[d, part],
                            (z * PEERS + other, t),
                        )
                    )
    for copy in large + small:
        copy.wait()
    for copy in [own_large] + own_small:
        copy.wait()
    for copy in list(ring.values()) + list(across.values()):
        copy.wait_send()


def shards(queries, key_head_states, value_head_states, output_gradient, doc_starts, span_map):
    anywhere = pl.BlockSpec(memory_space=pl.ANY)
    vmem = pl.BlockSpec(memory_space=pltpu.VMEM)
    hbm = pl.BlockSpec(memory_space=pltpu.HBM)
    dma = pltpu.SemaphoreType.DMA
    b16, f32 = jnp.bfloat16, jnp.float32
    wide = HEADS * WIDTH
    rows = PEERS * ROWS
    queries, output_gradient, key_head_states, value_head_states, span_map, doc_starts = (
        pltpu.with_memory_space_constraint(x, pltpu.HBM)
        for x in (queries, output_gradient, key_head_states, value_head_states, span_map, doc_starts)
    )
    grouped = jax.ShapeDtypeStruct((PEERS, ROWS, wide), b16)
    chunks = jax.ShapeDtypeStruct((2, RING, 2, rows, WIDTH), b16)
    qg, dog, kv = pl.pallas_call(
        gather_kernel,
        out_shape=(grouped, grouped, chunks),
        in_specs=[hbm] * 4,
        out_specs=(anywhere,) * 3,
        scratch_shapes=[
            dma((PEERS, 2)),
            dma((PEERS, 2)),
            dma((PEERS, 2)),
            dma((PEERS, 2)),
            dma((4, 2, 2, 2)),
            dma((4, 2, 2, 2)),
            dma((RING, 2, 2)),
            dma((RING, 2, 2)),
        ],
        compiler_params=pltpu.CompilerParams(
            collective_id=0, has_side_effects=True, vmem_limit_bytes=2 * 1024 * 1024
        ),
        name="gather_heads",
    )(queries, output_gradient, key_head_states, value_head_states)
    dqp, dkv = pl.pallas_call(
        attention_kernel,
        out_shape=(grouped, chunks),
        in_specs=[hbm, hbm, vmem, vmem, vmem],
        out_specs=(vmem, vmem),
        scratch_shapes=[
            pltpu.SMEM(span_map.shape, jnp.int32),
            pltpu.SMEM(doc_starts.shape, jnp.int32),
            pltpu.VMEM((KEYS + BLOCK, WIDTH), b16),
            pltpu.VMEM((KEYS + BLOCK, WIDTH), b16),
            pltpu.VMEM((WIDTH, KEYS + BLOCK), b16),
            pltpu.VMEM((KEYS + BLOCK, WIDTH), f32),
            pltpu.VMEM((KEYS + BLOCK, WIDTH), f32),
            pltpu.VMEM((STRETCH // BLOCK, BLOCK, HEADS * ROWS), f32),
            pltpu.VMEM((STRETCH // BLOCK, BLOCK, HEADS * ROWS), f32),
            pltpu.VMEM((STRETCH // BLOCK, 1, HEADS * ROWS), f32),
            pltpu.VMEM((WIDTH, HEADS * ROWS), f32),
            dma((2,)),
        ],
        compiler_params=pltpu.CompilerParams(vmem_limit_bytes=24 * 1024 * 1024),
        name="attention_grads",
    )(span_map, doc_starts, qg, dog, kv)
    return pl.pallas_call(
        scatter_kernel,
        out_shape=(
            jax.ShapeDtypeStruct((ROWS, PEERS * wide), b16),
            jax.ShapeDtypeStruct((ROWS, PEERS * WIDTH), b16),
            jax.ShapeDtypeStruct((ROWS, PEERS * WIDTH), b16),
        ),
        in_specs=[anywhere, vmem],
        out_specs=(anywhere,) * 3,
        scratch_shapes=[
            pltpu.VMEM((RING, 2, rows, WIDTH), b16),
            pltpu.VMEM((4, 2, 2, rows, WIDTH), b16),
            pltpu.VMEM((4, 2, 2, rows, WIDTH), b16),
            pltpu.VMEM((2, rows, WIDTH), b16),
            dma((RING,)),
            dma((RING,)),
            dma((PEERS,)),
            dma((PEERS,)),
            dma((4, 2, 2, 2)),
            dma((4, 2, 2, 2)),
            dma((PEERS, 2)),
            dma((PEERS, 2)),
        ],
        compiler_params=pltpu.CompilerParams(
            collective_id=1, has_side_effects=True, vmem_limit_bytes=12 * 1024 * 1024
        ),
        name="scatter_grads",
    )(dqp, dkv)


def solution(mesh):
    rows = P(("ctx", "tp"), None)
    in_specs = (rows, rows, rows, rows, P(), P())
    return jax.shard_map(
        shards, mesh=mesh, in_specs=in_specs, out_specs=(rows, rows, rows), check_vma=False
    )
```

time: 95 us -> 75.5 us (0.79)
  the two profiles are of different devices: /device:TPU:16 before, /device:TPU:8 now
where the time goes in v2:
time: 75.5 us; the launch traced here: 75.4 us
  Pallas kernels  72.6 us (96%)
  local copies, waits for them, and re-layouts  2.05 us (3%)
    pallas_call x1, Pallas kernels, shards(): pl.pallas_call(gather_kernel, out_shape=(grouped, grouped, chunks), in_sp...  30.3 us
    pallas_call x1, Pallas kernels, shards(): pl.pallas_call(scatter_kernel, out_shape=(jax.ShapeDtypeStruct((ROWS, PEE...  27.4 us
    pallas_call x1, Pallas kernels, shards(): pl.pallas_call(attention_kernel, out_shape=(grouped, chunks), in_specs=[h...  14.9 us
    unnamed x3, local copies, waits for them, and re-layouts  2.05 us

profile of v2, /device:TPU:8, one launch (start us, length us, event | category | flops | bytes accessed | tf_op | source)
XLA Modules:
  0.0 75.4 jit_solution(18018902887538777637)
XLA Ops:
  0.6 30.3 %gather_heads.1 = (bf16[8,32,1024]{2,1,0:T(8,128)(2,1)S(1)}, bf16[8,32,1024]{2,1,0:T(8,128)(2,1)S(1)}, bf16[2,8,2,256,128]{4,3,2,1,0:T(8,128)(2,1)S(1)}) custom-call(bf16[32,8192]{1,0:T(8,128)(2,1)} %q.1, bf16[32,8192]{1,0:T(8,128)(2,1)} %do.1, bf16[32,1024]{1,0:T(8,128)(2,1)} %k.1, bf16[32,1024]{1,0:T(8,128)(2,1)} %v.1), custom_call_target="tpu_custom_call" | custom-call | tf_op jit(solution)/shard_map/gather_heads/pallas_call | solution.py:387
  30.9 14.9 %attention_grads.1 = (bf16[8,32,1024]{2,1,0:T(8,128)(2,1)S(1)}, bf16[2,8,2,256,128]{4,3,2,1,0:T(8,128)(2,1)S(1)}) custom-call(s32[128]{0:T(128)} %spans_in.1, s32[16]{0:T(128)} %starts_in.1, bf16[8,32,1024]{2,1,0:T(8,128)(2,1)S(1)} %get-tuple-element.8.q, bf16[8,32,1024]{2,1,0:T(8,128)(2,1)S(1)} %get-tuple-element.9.do, ...), custom_call_target="tpu_custom_call" | custom-call | tf_op jit(solution)/shard_map/attention_grads/pallas_call | solution.py:407
  45.9 27.4 %scatter_grads.1 = (bf16[32,8192]{1,0:T(8,128)(2,1)S(1)}, bf16[32,1024]{1,0:T(8,128)(2,1)S(1)}, bf16[32,1024]{1,0:T(8,128)(2,1)S(1)}) custom-call(bf16[8,32,1024]{2,1,0:T(8,128)(2,1)S(1)} %get-tuple-element.11.dqp, bf16[2,8,2,256,128]{4,3,2,1,0:T(8,128)(2,1)S(1)} %get-tuple-element.12.dkv), custom_call_target="tpu_custom_call" | custom-call | tf_op jit(solution)/shard_map/scatter_grads/pallas_call | solution.py:429
  73.3 0.8 %copy.12 = bf16[32,8192]{1,0:T(8,128)(2,1)} copy(bf16[32,8192]{1,0:T(8,128)(2,1)S(1)} %get-tuple-element.16) | data formatting | bytes 1048576
  74.1 0.6 copy.13
  74.7 0.6 copy.14

commit v3 on v2

--- a/solution.py
+++ b/solution.py
@@ -16,8 +16,9 @@
 RING = 8
 SPAN = 64
 KEYS = 4096
-BLOCK = 512
-STRETCH = 2048
+BLOCK = 256
+TOGETHER = 6
+WORK = PEERS * 2048 // BLOCK
 SCALE = 1.0 / math.sqrt(WIDTH)
 SCALE_LOG2 = SCALE * math.log2(math.e)
 NEG_BIG = -1e30
@@ -149,7 +150,9 @@
 
 def attention_kernel(
     spans_in, starts_in, q, do, kv, dq, dkv,
-    spans, starts, key, value, key_t, dkey, dvalue, powers, dweights, tops, dq_t, sems,
+    spans, starts, work_tile, work_row, first_work,
+    key, value, dkey, dvalue, queries, grads, lows, highs,
+    powers, dweights, tops, totals, dots, tile_top, tile_inverse, tile_delta, dq_sum, sems,
 ):
     loads = [
         pltpu.make_async_copy(spans_in, spans, sems.at[0]),
@@ -167,10 +170,15 @@
         dvalue[rows] = jnp.zeros((BLOCK, WIDTH), jnp.float32)
         return 0
 
-    lax.fori_loop(0, KEYS // BLOCK, clear, 0)
+    lax.fori_loop(0, KEYS // BLOCK + 1, clear, 0)
     value[KEYS:] = jnp.zeros((BLOCK, WIDTH), jnp.bfloat16)
     key[KEYS:] = jnp.zeros((BLOCK, WIDTH), jnp.bfloat16)
-    key_t[:, KEYS:] = jnp.zeros((WIDTH, BLOCK), jnp.bfloat16)
+    dq_sum[...] = jnp.zeros_like(dq_sum)
+    for i in range(PEERS):
+        for h in range(HEADS):
+            part = slice(h * WIDTH, (h + 1) * WIDTH)
+            queries[i, h * ROWS : (h + 1) * ROWS] = q[i, :, part]
+            grads[i, h * ROWS : (h + 1) * ROWS] = do[i, :, part]
     for copy in loads:
         copy.wait()
 
@@ -187,22 +195,10 @@
 
     lax.fori_loop(0, RING, place_keys, 0)
 
-    def turn_keys(b, _):
-        rows = pl.ds(pl.multiple_of(b * BLOCK, BLOCK), BLOCK)
-        key_t[:, rows] = key[rows].T
-        return 0
-
-    lax.fori_loop(0, KEYS // BLOCK, turn_keys, 0)
     columns = HEADS * ROWS
 
-    def tile(i, _):
+    def plan(i, count):
         first = local_row(z * PEERS + i, core)
-        queries = jnp.concatenate(
-            [q[i, :, h * WIDTH : (h + 1) * WIDTH] for h in range(HEADS)], axis=0
-        )
-        grads = jnp.concatenate(
-            [do[i, :, h * WIDTH : (h + 1) * WIDTH] for h in range(HEADS)], axis=0
-        )
         row = first + lax.broadcasted_iota(jnp.int32, (1, columns), 1) % ROWS
         begin = jnp.int32(0)
         low = jnp.zeros((1, columns), jnp.int32)
@@ -210,56 +206,99 @@
             start = starts[n] - base
             begin = jnp.where(start <= first, jnp.maximum(begin, start), begin)
             low = jnp.where(start <= row, jnp.maximum(low, start), low)
+        lows[i] = low
+        highs[i] = row
         begin = (begin // WIDTH) * WIDTH
         steps = (first + ROWS - begin + BLOCK - 1) // BLOCK
-
-        def score_step(b, carry):
-            top, total, dot = carry
-            here = pl.multiple_of(begin + b * BLOCK, WIDTH)
+        first_work[i] = count
+
+        def enter(b, _):
+            work_tile[count + b] = i
+            work_row[count + b] = begin + b * BLOCK
+            return 0
+
+        lax.fori_loop(0, steps, enter, 0)
+        return count + steps
+
+    count = lax.fori_loop(0, PEERS, plan, jnp.int32(0))
+    first_work[PEERS] = count
+    for u in range(TOGETHER - 1):
+        work_tile[count + u] = 0
+        work_row[count + u] = KEYS
+    groups = (count + TOGETHER - 1) // TOGETHER
+
+    def score_group(g, _):
+        products = []
+        for u in range(TOGETHER):
+            n = g * TOGETHER + u
+            i = work_tile[n]
+            here = pl.multiple_of(work_row[n], WIDTH)
             rows = pl.ds(here, BLOCK)
             s = lax.dot_general(
-                key[rows], queries, (((1,), (1,)), ((), ())), preferred_element_type=jnp.float32
+                key[rows], queries[i], (((1,), (1,)), ((), ())), preferred_element_type=jnp.float32
             )
             dw = lax.dot_general(
-                value[rows], grads, (((1,), (1,)), ((), ())), preferred_element_type=jnp.float32
+                value[rows], grads[i], (((1,), (1,)), ((), ())), preferred_element_type=jnp.float32
             )
-            dweights[b] = dw
+            products.append((here, lows[i], highs[i], s, dw))
+        for u, (here, low, high, s, dw) in enumerate(products):
+            n = g * TOGETHER + u
             pos = here + lax.broadcasted_iota(jnp.int32, (BLOCK, columns), 0)
-            s = jnp.where((pos >= low) & (pos <= row), s * SCALE_LOG2, NEG_BIG)
-            new = jnp.maximum(top, jnp.max(s, axis=0, keepdims=True))
-            e = jnp.exp2(s - new)
-            powers[b] = e
-            tops[b] = new
-            factor = jnp.exp2(top - new)
-            total = total * factor + jnp.sum(e, axis=0, keepdims=True)
-            dot = dot * factor + jnp.sum(e * dw, axis=0, keepdims=True)
-            return new, total, dot
-
-        zero = jnp.zeros((1, columns), jnp.float32)
-        top, total, dot = lax.fori_loop(0, steps, score_step, (zero + NEG_BIG, zero, zero))
+            s = jnp.where((pos - low).astype(jnp.uint32) <= (high - low).astype(jnp.uint32), s * SCALE_LOG2, NEG_BIG)
+            top = jnp.max(s, axis=0, keepdims=True)
+            e = jnp.exp2(s - top)
+            dweights[n] = dw
+            powers[n] = s
+            tops[pl.ds(n, 1)] = top
+            totals[pl.ds(n, 1)] = jnp.sum(e, axis=0, keepdims=True)
+            dots[pl.ds(n, 1)] = jnp.sum(e * dw, axis=0, keepdims=True)
+        return 0
+
+    lax.fori_loop(0, groups, score_group, 0)
+    entry = lax.broadcasted_iota(jnp.int32, (WORK, 1), 0)
+    for i in range(PEERS):
+        mine = (entry >= first_work[i]) & (entry < first_work[i + 1])
+        tops_i = jnp.where(mine, tops[:WORK], NEG_BIG)
+        top = jnp.max(tops_i, axis=0, keepdims=True)
+        factor = jnp.exp2(tops_i - top)
+        total = jnp.sum(jnp.where(mine, totals[:WORK] * factor, 0.0), axis=0, keepdims=True)
+        dot = jnp.sum(jnp.where(mine, dots[:WORK] * factor, 0.0), axis=0, keepdims=True)
         inverse = 1.0 / total
-        delta = dot * inverse
-        dq_t[...] = jnp.zeros_like(dq_t)
-
-        def grad_step(b, _):
-            here = pl.multiple_of(begin + b * BLOCK, WIDTH)
-            rows = pl.ds(here, BLOCK)
-            w = powers[b] * (jnp.exp2(tops[b] - top) * inverse)
-            ds = (w * (dweights[b] - delta)).astype(jnp.bfloat16)
-            dvalue[rows] += jnp.dot(
-                w.astype(jnp.bfloat16), grads, preferred_element_type=jnp.float32
+        tile_top[i] = top + jnp.log2(total)
+        tile_inverse[i] = inverse
+        tile_delta[i] = dot * inverse
+
+    def grad_group(g, _):
+        products = []
+        for u in range(TOGETHER):
+            n = g * TOGETHER + u
+            i = work_tile[n]
+            rows = pl.ds(pl.multiple_of(work_row[n], WIDTH), BLOCK)
+            w = jnp.exp2(powers[n] - tile_top[i])
+            ds = (w * (dweights[n] - tile_delta[i])).astype(jnp.bfloat16)
+            w = w.astype(jnp.bfloat16)
+            products.append(
+                (
+                    i,
+                    rows,
+                    jnp.dot(w, grads[i], preferred_element_type=jnp.float32),
+                    jnp.dot(ds, queries[i], preferred_element_type=jnp.float32),
+                    lax.dot_general(
+                        ds, key[rows], (((0,), (0,)), ((), ())), preferred_element_type=jnp.float32
+                    ),
+                )
             )
-            dkey[rows] += jnp.dot(ds, queries, preferred_element_type=jnp.float32)
-            dq_t[...] += jnp.dot(key_t[:, rows], ds, preferred_element_type=jnp.float32)
-            return 0
-
-        lax.fori_loop(0, steps, grad_step, 0)
-        out = (dq_t[...] * SCALE).T.astype(jnp.bfloat16)
+        for i, rows, to_value, to_key, to_query in products:
+            dvalue[rows] += to_value
+            dkey[rows] += to_key
+            dq_sum[i] += to_query
+        return 0
+
+    lax.fori_loop(0, groups, grad_group, 0)
+    for i in range(PEERS):
+        out = (dq_sum[i] * SCALE).astype(jnp.bfloat16)
         for h in range(HEADS):
             dq[i, :, h * WIDTH : (h + 1) * WIDTH] = out[h * ROWS : (h + 1) * ROWS]
-        return 0
-
-    lax.fori_loop(0, PEERS, tile, 0)
 
     def give_keys(i, _):
         for j in range(PEERS):
@@ -370,21 +409,61 @@
         copy.wait_send()
 
 
-def shards(queries, key_head_states, value_head_states, output_gradient, doc_starts, span_map):
+def attend(span_map, doc_starts, qg, dog, kv):
+    vmem = pl.BlockSpec(memory_space=pltpu.VMEM)
+    hbm = pl.BlockSpec(memory_space=pltpu.HBM)
+    dma = pltpu.SemaphoreType.DMA
+    b16, f32 = jnp.bfloat16, jnp.float32
+    columns = HEADS * ROWS
+    return pl.pallas_call(
+        attention_kernel,
+        out_shape=(
+            jax.ShapeDtypeStruct(qg.shape, b16),
+            jax.ShapeDtypeStruct(kv.shape, b16),
+        ),
+        in_specs=[hbm, hbm, vmem, vmem, vmem],
+        out_specs=(vmem, vmem),
+        scratch_shapes=[
+            pltpu.SMEM(span_map.shape, jnp.int32),
+            pltpu.SMEM(doc_starts.shape, jnp.int32),
+            pltpu.SMEM((WORK + TOGETHER,), jnp.int32),
+            pltpu.SMEM((WORK + TOGETHER,), jnp.int32),
+            pltpu.SMEM((PEERS + 1,), jnp.int32),
+            pltpu.VMEM((KEYS + BLOCK, WIDTH), b16),
+            pltpu.VMEM((KEYS + BLOCK, WIDTH), b16),
+            pltpu.VMEM((KEYS + BLOCK, WIDTH), f32),
+            pltpu.VMEM((KEYS + BLOCK, WIDTH), f32),
+            pltpu.VMEM((PEERS, columns, WIDTH), b16),
+            pltpu.VMEM((PEERS, columns, WIDTH), b16),
+            pltpu.VMEM((PEERS, 1, columns), jnp.int32),
+            pltpu.VMEM((PEERS, 1, columns), jnp.int32),
+            pltpu.VMEM((WORK + TOGETHER, BLOCK, columns), f32),
+            pltpu.VMEM((WORK + TOGETHER, BLOCK, columns), f32),
+            pltpu.VMEM((WORK + 8, columns), f32),
+            pltpu.VMEM((WORK + 8, columns), f32),
+            pltpu.VMEM((WORK + 8, columns), f32),
+            pltpu.VMEM((PEERS, 1, columns), f32),
+            pltpu.VMEM((PEERS, 1, columns), f32),
+            pltpu.VMEM((PEERS, 1, columns), f32),
+            pltpu.VMEM((PEERS, columns, WIDTH), f32),
+            dma((2,)),
+        ],
+        compiler_params=pltpu.CompilerParams(vmem_limit_bytes=48 * 1024 * 1024),
+        name="attention_grads",
+    )(span_map, doc_starts, qg, dog, kv)
+
+
+def gather(queries, output_gradient, key_head_states, value_head_states):
     anywhere = pl.BlockSpec(memory_space=pl.ANY)
     vmem = pl.BlockSpec(memory_space=pltpu.VMEM)
     hbm = pl.BlockSpec(memory_space=pltpu.HBM)
     dma = pltpu.SemaphoreType.DMA
-    b16, f32 = jnp.bfloat16, jnp.float32
+    b16 = jnp.bfloat16
     wide = HEADS * WIDTH
     rows = PEERS * ROWS
-    queries, output_gradient, key_head_states, value_head_states, span_map, doc_starts = (
-        pltpu.with_memory_space_constraint(x, pltpu.HBM)
-        for x in (queries, output_gradient, key_head_states, value_head_states, span_map, doc_starts)
-    )
     grouped = jax.ShapeDtypeStruct((PEERS, ROWS, wide), b16)
     chunks = jax.ShapeDtypeStruct((2, RING, 2, rows, WIDTH), b16)
-    qg, dog, kv = pl.pallas_call(
+    return pl.pallas_call(
         gather_kernel,
         out_shape=(grouped, grouped, chunks),
         in_specs=[hbm] * 4,
@@ -404,28 +483,16 @@
         ),
         name="gather_heads",
     )(queries, output_gradient, key_head_states, value_head_states)
-    dqp, dkv = pl.pallas_call(
-        attention_kernel,
-        out_shape=(grouped, chunks),
-        in_specs=[hbm, hbm, vmem, vmem, vmem],
-        out_specs=(vmem, vmem),
-        scratch_shapes=[
-            pltpu.SMEM(span_map.shape, jnp.int32),
-            pltpu.SMEM(doc_starts.shape, jnp.int32),
-            pltpu.VMEM((KEYS + BLOCK, WIDTH), b16),
-            pltpu.VMEM((KEYS + BLOCK, WIDTH), b16),
-            pltpu.VMEM((WIDTH, KEYS + BLOCK), b16),
-            pltpu.VMEM((KEYS + BLOCK, WIDTH), f32),
-            pltpu.VMEM((KEYS + BLOCK, WIDTH), f32),
-            pltpu.VMEM((STRETCH // BLOCK, BLOCK, HEADS * ROWS), f32),
-            pltpu.VMEM((STRETCH // BLOCK, BLOCK, HEADS * ROWS), f32),
-            pltpu.VMEM((STRETCH // BLOCK, 1, HEADS * ROWS), f32),
-            pltpu.VMEM((WIDTH, HEADS * ROWS), f32),
-            dma((2,)),
-        ],
-        compiler_params=pltpu.CompilerParams(vmem_limit_bytes=24 * 1024 * 1024),
-        name="attention_grads",
-    )(span_map, doc_starts, qg, dog, kv)
+
+
+def scatter(dqp, dkv):
+    anywhere = pl.BlockSpec(memory_space=pl.ANY)
+    vmem = pl.BlockSpec(memory_space=pltpu.VMEM)
+    hbm = pl.BlockSpec(memory_space=pltpu.HBM)
+    dma = pltpu.SemaphoreType.DMA
+    b16 = jnp.bfloat16
+    wide = HEADS * WIDTH
+    rows = PEERS * ROWS
     return pl.pallas_call(
         scatter_kernel,
         out_shape=(
@@ -456,6 +523,41 @@
     )(dqp, dkv)
 
 
+def finish_kernel(dq_in, dk_in, dv_in, dq, dk, dv, sems):
+    copies = [
+        pltpu.make_async_copy(src, dst, sems.at[n])
+        for n, (src, dst) in enumerate(((dq_in, dq), (dk_in, dk), (dv_in, dv)))
+    ]
+    for copy in copies:
+        copy.start()
+    for copy in copies:
+        copy.wait()
+
+
+def finish(*grads):
+    anywhere = pl.BlockSpec(memory_space=pl.ANY)
+    hbm = pl.BlockSpec(memory_space=pltpu.HBM)
+    return pl.pallas_call(
+        finish_kernel,
+        out_shape=tuple(jax.ShapeDtypeStruct(x.shape, x.dtype) for x in grads),
+        in_specs=[anywhere] * 3,
+        out_specs=(hbm,) * 3,
+        scratch_shapes=[pltpu.SemaphoreType.DMA((3,))],
+        compiler_params=pltpu.CompilerParams(vmem_limit_bytes=1024 * 1024),
+        name="finish",
+    )(*grads)
+
+
+def shards(queries, key_head_states, value_head_states, output_gradient, doc_starts, span_map):
+    queries, output_gradient, key_head_states, value_head_states, span_map, doc_starts = (
+        pltpu.with_memory_space_constraint(x, pltpu.HBM)
+        for x in (queries, output_gradient, key_head_states, value_head_states, span_map, doc_starts)
+    )
+    qg, dog, kv = gather(queries, output_gradient, key_head_states, value_head_states)
+    dqp, dkv = attend(span_map, doc_starts, qg, dog, kv)
+    return finish(*scatter(dqp, dkv))
+
+
 def solution(mesh):
     rows = P(("ctx", "tp"), None)
     in_specs = (rows, rows, rows, rows, P(), P())

time: 75.5 us -> 68.9 us (0.913)
  Pallas kernels: 72.6 us -> 68.1 us
  local copies, waits for them, and re-layouts: 2.05 us -> 0 us
    pallas_call x3 -> x4, Pallas kernels: 72.6 us -> 68.1 us  [the longest x1 30.3 us: gather(): pl.pallas_call(gather_kernel, out_shape=(grouped, grouped, chunks), in_sp...]
    unnamed x3 -> x0, local copies, waits for them, and re-layouts: 2.05 us -> none
where the time goes in v3:
time: 68.9 us; the launch traced here: 68.7 us
  Pallas kernels  68.1 us (99%)
    pallas_call x1, Pallas kernels, gather(): pl.pallas_call(gather_kernel, out_shape=(grouped, grouped, chunks), in_sp...  30.3 us
    pallas_call x1, Pallas kernels, scatter(): pl.pallas_call(scatter_kernel, out_shape=(jax.ShapeDtypeStruct((ROWS, PEE...  26.2 us
    pallas_call x1, Pallas kernels, attend(): pl.pallas_call(attention_kernel, out_shape=(jax.ShapeDtypeStruct(qg.shape...  10.8 us

profile of v3, /device:TPU:8, one launch (start us, length us, event | category | flops | bytes accessed | tf_op | source)
XLA Modules:
  0.0 68.7 jit_solution(1930863909156775071)
XLA Ops:
  0.6 30.3 %gather_heads.1 = (bf16[8,32,1024]{2,1,0:T(8,128)(2,1)S(1)}, bf16[8,32,1024]{2,1,0:T(8,128)(2,1)S(1)}, bf16[2,8,2,256,128]{4,3,2,1,0:T(8,128)(2,1)S(1)}) custom-call(bf16[32,8192]{1,0:T(8,128)(2,1)} %q.1, bf16[32,8192]{1,0:T(8,128)(2,1)} %do.1, bf16[32,1024]{1,0:T(8,128)(2,1)} %k.1, bf16[32,1024]{1,0:T(8,128)(2,1)} %v.1), custom_call_target="tpu_custom_call" | custom-call | tf_op jit(solution)/shard_map/gather_heads/pallas_call | solution.py:466
  30.9 10.8 %attention_grads.1 = (bf16[8,32,1024]{2,1,0:T(8,128)(2,1)S(1)}, bf16[2,8,2,256,128]{4,3,2,1,0:T(8,128)(2,1)S(1)}) custom-call(s32[128]{0:T(128)} %spans_in.1, s32[16]{0:T(128)} %starts_in.1, bf16[8,32,1024]{2,1,0:T(8,128)(2,1)S(1)} %get-tuple-element.11.q, bf16[8,32,1024]{2,1,0:T(8,128)(2,1)S(1)} %get-tuple-element.12.do, ...), custom_call_target="tpu_custom_call" | custom-call | tf_op jit(solution)/shard_map/attention_grads/pallas_call | solution.py:418
  41.7 26.2 %scatter_grads.1 = (bf16[32,8192]{1,0:T(8,128)(2,1)S(1)}, bf16[32,1024]{1,0:T(8,128)(2,1)S(1)}, bf16[32,1024]{1,0:T(8,128)(2,1)S(1)}) custom-call(bf16[8,32,1024]{2,1,0:T(8,128)(2,1)S(1)} %get-tuple-element.14.dqp, bf16[2,8,2,256,128]{4,3,2,1,0:T(8,128)(2,1)S(1)} %get-tuple-element.15.dkv), custom_call_target="tpu_custom_call" | custom-call | tf_op jit(solution)/shard_map/scatter_grads/pallas_call | solution.py:496
  67.9 0.9 %finish.1 = (bf16[32,8192]{1,0:T(8,128)(2,1)}, bf16[32,1024]{1,0:T(8,128)(2,1)}, bf16[32,1024]{1,0:T(8,128)(2,1)}) custom-call(bf16[32,8192]{1,0:T(8,128)(2,1)S(1)} %get-tuple-element.16.dq_in, bf16[32,1024]{1,0:T(8,128)(2,1)S(1)} %get-tuple-element.17.dk_in, bf16[32,1024]{1,0:T(8,128)(2,1)S(1)} %get-tuple-element.18.dv_in), custom_call_target="tpu_custom_call" | custom-call | tf_op jit(solution)/shard_map/finish/pallas_call | solution.py:540

commit v4 on v3

--- a/solution.py
+++ b/solution.py
@@ -38,13 +38,24 @@
     return pl.ds(pl.multiple_of(((p // 4 + half) % 2) * rows, rows), rows)
 
 
-def greet(z, p, t, right, left, sibling):
+def beside(z, p, t, way, far):
+    return along_z(z, p, far if way == 0 else RING - far), t
+
+
+def along_z(z, p, offset):
+    return ((z + offset) % RING) * PEERS + p
+
+
+def greet(z, p, t, sibling, row):
     barrier = pltpu.get_barrier_semaphore()
-    targets = [(z * PEERS + peer_of(p, d), t) for d in range(1, PEERS)]
-    targets += [(right, t), (left, t), (z * PEERS + p, sibling)]
+    targets = [(z * PEERS + peer_of(p, d), t) for d in range(1, PEERS // 2 + 1)]
+    targets += [(along_z(z, p, offset), t) for offset in (1, 2, RING - 2, RING - 1)]
+    targets.append((z * PEERS + p, sibling))
     for target in targets:
         pl.semaphore_signal(barrier, inc=1, device_id=target, device_id_type=MESH)
     pl.semaphore_wait(barrier, len(targets))
+    across = (z * PEERS + peer_of(p, PEERS // 2), t)
+    pl.semaphore_signal(row, inc=1, device_id=across, device_id_type=MESH)
 
 
 def remote(src, dst, send, recv, target):
@@ -56,13 +67,12 @@
 
 
 def gather_kernel(
-    q, do, k, v, qg, dog, kv, kv_s, kv_r, q_s, q_r, ring_s, ring_r, sib_s, sib_r
+    q, do, k, v, qg, dog, kv, kv_s, kv_r, q_s, q_r, ring_s, ring_r, sib_s, sib_r, row
 ):
     z, p, t, y_lo, core = place()
-    right, left = ((z + 1) % RING) * PEERS + p, ((z + RING - 1) % RING) * PEERS + p
     here = z * PEERS + p
     sibling = y_lo * 2 + 1 - core
-    greet(z, p, t, right, left, sibling)
+    greet(z, p, t, sibling, row)
     small, large, ring, across, own = {}, [], {}, [], []
     for part, src in enumerate((k, v)):
         copy = pltpu.make_async_copy(
@@ -74,6 +84,8 @@
         own.append(copy)
     for d in ORDER:
         other = peer_of(p, d)
+        if d == PEERS // 2:
+            pl.semaphore_wait(row, 1)
         for part, src in enumerate((k, v)):
             small[d, part] = remote(
                 src.at[:, pl.ds(pl.multiple_of(other * WIDTH, WIDTH), WIDTH)],
@@ -109,7 +121,7 @@
     def forward(step, way, part, half, offset):
         chunk = piece(part, half, offset)
         key = step, way, part, half
-        target = (right if way == 0 else left, t)
+        target = beside(z, p, t, way, 2 if step == 3 else 1)
         ring[key] = remote(chunk, chunk, ring_s.at[key], ring_r.at[key], target)
 
     def share(part, half, offset):
@@ -135,8 +147,10 @@
                         continue
                     offset = RING - step if way == 0 else step
                     ring[step - 1, way, part, half].wait_recv()
-                    if step < 3 or (step == 3 and way == part):
+                    if step < 3:
                         forward(step, way, part, half, offset)
+                    if step == 2 and way == part:
+                        forward(3, way, part, half, offset)
                     share(part, half, offset)
     for copy in across:
         copy.wait_recv()
@@ -314,14 +328,13 @@
 
 def scatter_kernel(
     dqp, dkv, dq, dk, dv, pair, got, sent, final,
-    pair_s, pair_r, q_s, q_r, ring_s, ring_r, kv_s, kv_r,
+    pair_s, pair_r, q_s, q_r, ring_s, ring_r, kv_s, kv_r, row,
 ):
     z, p, t, y_lo, core = place()
-    right, left = ((z + 1) % RING) * PEERS + p, ((z + RING - 1) % RING) * PEERS + p
     here = z * PEERS + p
     sibling = y_lo * 2 + 1 - core
     across, large, ring, small = {}, [], {}, []
-    greet(z, p, t, right, left, sibling)
+    greet(z, p, t, sibling, row)
     for offset in (4, 3, 5, 2, 6, 1, 7, 0):
         across[offset] = remote(
             dkv.at[1 - core, (z + offset) % RING],
@@ -330,17 +343,6 @@
             pair_r.at[offset],
             (here, sibling),
         )
-    wide = HEADS * WIDTH
-    columns = pl.ds(pl.multiple_of(p * wide, wide), wide)
-    for d in ORDER:
-        other = peer_of(p, d)
-        large.append(
-            remote(
-                dqp.at[other], dq.at[:, columns], q_s.at[d], q_r.at[d], (z * PEERS + other, t)
-            )
-        )
-    own_large = pltpu.make_async_copy(dqp.at[p], dq.at[:, columns], q_s.at[0])
-    own_large.start()
     met = set()
 
     def term(offset, part, half):
@@ -355,32 +357,51 @@
         ring[step, way, part, half].wait_recv()
         return got[step, way, part, half_rows(p, half)].astype(jnp.float32)
 
-    for step in range(4):
+    def send(step, way, part, half, value):
+        rows = half_rows(p, half)
+        key = step, way, part, half
+        sent[step, way, part, rows] = value.astype(jnp.bfloat16)
+        ring[key] = remote(
+            sent.at[step, way, part, rows],
+            got.at[step, way, part, rows],
+            ring_s.at[key],
+            ring_r.at[key],
+            beside(z, p, t, way, 2 if step == 3 else 1),
+        )
+
+    for step in range(3):
         for half in (1, 0):
+            if step == 0:
+                for way in range(2):
+                    send(3, way, way, half, term(4, way, half))
             for part in range(2):
                 for way in range(2):
-                    if step == 0 and part != way:
-                        continue
-                    value = term(4 - step if way == 0 else 4 + step, part, half)
-                    if step > 1 or (step == 1 and part == way):
+                    value = term(3 - step if way == 0 else RING - 3 + step, part, half)
+                    if step > 0:
                         value += arrived(step - 1, way, part, half)
-                    rows = half_rows(p, half)
-                    key = step, way, part, half
-                    sent[step, way, part, rows] = value.astype(jnp.bfloat16)
-                    ring[key] = remote(
-                        sent.at[step, way, part, rows],
-                        got.at[step, way, part, rows],
-                        ring_s.at[key],
-                        ring_r.at[key],
-                        (right if way == 0 else left, t),
+                    if step == 1 and part == way:
+                        value += arrived(3, way, part, half)
+                    send(step, way, part, half, value)
+        if step == 0:
+            pl.semaphore_wait(row, 1)
+            wide = HEADS * WIDTH
+            columns = pl.ds(pl.multiple_of(p * wide, wide), wide)
+            for d in ORDER:
+                other = peer_of(p, d)
+                large.append(
+                    remote(
+                        dqp.at[other], dq.at[:, columns], q_s.at[d], q_r.at[d], (z * PEERS + other, t)
                     )
+                )
+            own_large = pltpu.make_async_copy(dqp.at[p], dq.at[:, columns], q_s.at[0])
+            own_large.start()
     narrow = pl.ds(pl.multiple_of(p * WIDTH, WIDTH), WIDTH)
     own_small = []
     for half in (1, 0):
         for part, dst in enumerate((dk, dv)):
             value = term(0, part, half)
             for way in range(2):
-                value += arrived(3, way, part, half)
+                value += arrived(2, way, part, half)
             final[part, half_rows(p, half)] = value.astype(jnp.bfloat16)
             for d in range(PEERS):
                 if d // 4 != half:
@@ -477,6 +498,7 @@
             dma((4, 2, 2, 2)),
             dma((RING, 2, 2)),
             dma((RING, 2, 2)),
+            pltpu.SemaphoreType.REGULAR,
         ],
         compiler_params=pltpu.CompilerParams(
             collective_id=0, has_side_effects=True, vmem_limit_bytes=2 * 1024 * 1024
@@ -515,6 +537,7 @@
             dma((4, 2, 2, 2)),
             dma((PEERS, 2)),
             dma((PEERS, 2)),
+            pltpu.SemaphoreType.REGULAR,
         ],
         compiler_params=pltpu.CompilerParams(
             collective_id=1, has_side_effects=True, vmem_limit_bytes=12 * 1024 * 1024

time: 68.9 us -> 68 us (0.987)
  Pallas kernels: 68.1 us -> 67.2 us
    pallas_call x1, Pallas kernels: 30.3 us -> 29.5 us  [gather(): pl.pallas_call(gather_kernel, out_shape=(grouped, grouped, chunks), in_sp...]
where the time goes in v4:
time: 68 us; the launch traced here: 67.9 us
  Pallas kernels  67.2 us (99%)
    pallas_call x1, Pallas kernels, gather(): pl.pallas_call(gather_kernel, out_shape=(grouped, grouped, chunks), in_sp...  29.5 us
    pallas_call x1, Pallas kernels, scatter(): pl.pallas_call(scatter_kernel, out_shape=(jax.ShapeDtypeStruct((ROWS, PEE...  26.2 us
    pallas_call x1, Pallas kernels, attend(): pl.pallas_call(attention_kernel, out_shape=(jax.ShapeDtypeStruct(qg.shape...  10.7 us

profile of v4, /device:TPU:8, one launch (start us, length us, event | category | flops | bytes accessed | tf_op | source)
XLA Modules:
  0.0 67.9 jit_solution(7930918510481575405)
XLA Ops:
  0.6 29.5 %gather_heads.1 = (bf16[8,32,1024]{2,1,0:T(8,128)(2,1)S(1)}, bf16[8,32,1024]{2,1,0:T(8,128)(2,1)S(1)}, bf16[2,8,2,256,128]{4,3,2,1,0:T(8,128)(2,1)S(1)}) custom-call(bf16[32,8192]{1,0:T(8,128)(2,1)} %q.1, bf16[32,8192]{1,0:T(8,128)(2,1)} %do.1, bf16[32,1024]{1,0:T(8,128)(2,1)} %k.1, bf16[32,1024]{1,0:T(8,128)(2,1)} %v.1), custom_call_target="tpu_custom_call" | custom-call | tf_op jit(solution)/shard_map/gather_heads/pallas_call | solution.py:487
  30.1 10.7 %attention_grads.1 = (bf16[8,32,1024]{2,1,0:T(8,128)(2,1)S(1)}, bf16[2,8,2,256,128]{4,3,2,1,0:T(8,128)(2,1)S(1)}) custom-call(s32[128]{0:T(128)} %spans_in.1, s32[16]{0:T(128)} %starts_in.1, bf16[8,32,1024]{2,1,0:T(8,128)(2,1)S(1)} %get-tuple-element.11.q, bf16[8,32,1024]{2,1,0:T(8,128)(2,1)S(1)} %get-tuple-element.12.do, ...), custom_call_target="tpu_custom_call" | custom-call | tf_op jit(solution)/shard_map/attention_grads/pallas_call | solution.py:439
  40.8 26.2 %scatter_grads.1 = (bf16[32,8192]{1,0:T(8,128)(2,1)S(1)}, bf16[32,1024]{1,0:T(8,128)(2,1)S(1)}, bf16[32,1024]{1,0:T(8,128)(2,1)S(1)}) custom-call(bf16[8,32,1024]{2,1,0:T(8,128)(2,1)S(1)} %get-tuple-element.14.dqp, bf16[2,8,2,256,128]{4,3,2,1,0:T(8,128)(2,1)S(1)} %get-tuple-element.15.dkv), custom_call_target="tpu_custom_call" | custom-call | tf_op jit(solution)/shard_map/scatter_grads/pallas_call | solution.py:518
  67.0 0.9 %finish.1 = (bf16[32,8192]{1,0:T(8,128)(2,1)}, bf16[32,1024]{1,0:T(8,128)(2,1)}, bf16[32,1024]{1,0:T(8,128)(2,1)}) custom-call(bf16[32,8192]{1,0:T(8,128)(2,1)S(1)} %get-tuple-element.16.dq_in, bf16[32,1024]{1,0:T(8,128)(2,1)S(1)} %get-tuple-element.17.dk_in, bf16[32,1024]{1,0:T(8,128)(2,1)S(1)} %get-tuple-element.18.dv_in), custom_call_target="tpu_custom_call" | custom-call | tf_op jit(solution)/shard_map/finish/pallas_call | solution.py:563

commit v5 on v4

--- a/solution.py
+++ b/solution.py
@@ -17,8 +17,9 @@
 SPAN = 64
 KEYS = 4096
 BLOCK = 256
-TOGETHER = 6
-WORK = PEERS * 2048 // BLOCK
+CLEAR = 64
+TOGETHER = 7
+WORK = PEERS * -(-2048 // BLOCK)
 SCALE = 1.0 / math.sqrt(WIDTH)
 SCALE_LOG2 = SCALE * math.log2(math.e)
 NEG_BIG = -1e30
@@ -179,12 +180,12 @@
     base = y_lo * KEYS
 
     def clear(b, _):
-        rows = pl.ds(pl.multiple_of(b * BLOCK, BLOCK), BLOCK)
-        dkey[rows] = jnp.zeros((BLOCK, WIDTH), jnp.float32)
-        dvalue[rows] = jnp.zeros((BLOCK, WIDTH), jnp.float32)
+        rows = pl.ds(pl.multiple_of(b * CLEAR, CLEAR), CLEAR)
+        dkey[rows] = jnp.zeros((CLEAR, WIDTH), jnp.float32)
+        dvalue[rows] = jnp.zeros((CLEAR, WIDTH), jnp.float32)
         return 0
 
-    lax.fori_loop(0, KEYS // BLOCK + 1, clear, 0)
+    lax.fori_loop(0, (KEYS + BLOCK) // CLEAR, clear, 0)
     value[KEYS:] = jnp.zeros((BLOCK, WIDTH), jnp.bfloat16)
     key[KEYS:] = jnp.zeros((BLOCK, WIDTH), jnp.bfloat16)
     dq_sum[...] = jnp.zeros_like(dq_sum)
@@ -222,7 +223,7 @@
             low = jnp.where(start <= row, jnp.maximum(low, start), low)
         lows[i] = low
         highs[i] = row
-        begin = (begin // WIDTH) * WIDTH
+        begin = (begin // ROWS) * ROWS
         steps = (first + ROWS - begin + BLOCK - 1) // BLOCK
         first_work[i] = count
 
@@ -234,7 +235,9 @@
         lax.fori_loop(0, steps, enter, 0)
         return count + steps
 
-    count = lax.fori_loop(0, PEERS, plan, jnp.int32(0))
+    count = jnp.int32(0)
+    for i in range(PEERS):
+        count = plan(i, count)
     first_work[PEERS] = count
     for u in range(TOGETHER - 1):
         work_tile[count + u] = 0
@@ -246,7 +249,7 @@
         for u in range(TOGETHER):
             n = g * TOGETHER + u
             i = work_tile[n]
-            here = pl.multiple_of(work_row[n], WIDTH)
+            here = pl.multiple_of(work_row[n], ROWS)
             rows = pl.ds(here, BLOCK)
             s = lax.dot_general(
                 key[rows], queries[i], (((1,), (1,)), ((), ())), preferred_element_type=jnp.float32
@@ -287,7 +290,7 @@
         for u in range(TOGETHER):
             n = g * TOGETHER + u
             i = work_tile[n]
-            rows = pl.ds(pl.multiple_of(work_row[n], WIDTH), BLOCK)
+            rows = pl.ds(pl.multiple_of(work_row[n], ROWS), BLOCK)
             w = jnp.exp2(powers[n] - tile_top[i])
             ds = (w * (dweights[n] - tile_delta[i])).astype(jnp.bfloat16)
             w = w.astype(jnp.bfloat16)
@@ -460,9 +463,9 @@
             pltpu.VMEM((PEERS, 1, columns), jnp.int32),
             pltpu.VMEM((WORK + TOGETHER, BLOCK, columns), f32),
             pltpu.VMEM((WORK + TOGETHER, BLOCK, columns), f32),
-            pltpu.VMEM((WORK + 8, columns), f32),
-            pltpu.VMEM((WORK + 8, columns), f32),
-            pltpu.VMEM((WORK + 8, columns), f32),
+            pltpu.VMEM((WORK + 8 + TOGETHER, columns), f32),
+            pltpu.VMEM((WORK + 8 + TOGETHER, columns), f32),
+            pltpu.VMEM((WORK + 8 + TOGETHER, columns), f32),
             pltpu.VMEM((PEERS, 1, columns), f32),
             pltpu.VMEM((PEERS, 1, columns), f32),
             pltpu.VMEM((PEERS, 1, columns), f32),

time: 68 us -> 65.8 us (0.968)
  Pallas kernels: 67.2 us -> 65.2 us
    pallas_call x1, Pallas kernels: 10.7 us -> 8.04 us  [attend(): pl.pallas_call(attention_kernel, out_shape=(jax.ShapeDtypeStruct(qg.shape...]
where the time goes in v5:
time: 65.8 us
  Pallas kernels  65.2 us (99%)
    pallas_call x1, Pallas kernels, gather(): pl.pallas_call(gather_kernel, out_shape=(grouped, grouped, chunks), in_sp...  29.5 us
    pallas_call x1, Pallas kernels, scatter(): pl.pallas_call(scatter_kernel, out_shape=(jax.ShapeDtypeStruct((ROWS, PEE...  26.8 us
    pallas_call x1, Pallas kernels, attend(): pl.pallas_call(attention_kernel, out_shape=(jax.ShapeDtypeStruct(qg.shape...  8.04 us

profile of v5, /device:TPU:8, one launch (start us, length us, event | category | flops | bytes accessed | tf_op | source)
XLA Modules:
  0.0 65.8 jit_solution(17200701639779262233)
XLA Ops:
  0.6 29.5 %gather_heads.1 = (bf16[8,32,1024]{2,1,0:T(8,128)(2,1)S(1)}, bf16[8,32,1024]{2,1,0:T(8,128)(2,1)S(1)}, bf16[2,8,2,256,128]{4,3,2,1,0:T(8,128)(2,1)S(1)}) custom-call(bf16[32,8192]{1,0:T(8,128)(2,1)} %q.1, bf16[32,8192]{1,0:T(8,128)(2,1)} %do.1, bf16[32,1024]{1,0:T(8,128)(2,1)} %k.1, bf16[32,1024]{1,0:T(8,128)(2,1)} %v.1), custom_call_target="tpu_custom_call" | custom-call | tf_op jit(solution)/shard_map/gather_heads/pallas_call | solution.py:490
  30.1 8.0 %attention_grads.1 = (bf16[8,32,1024]{2,1,0:T(8,128)(2,1)S(1)}, bf16[2,8,2,256,128]{4,3,2,1,0:T(8,128)(2,1)S(1)}) custom-call(s32[128]{0:T(128)} %spans_in.1, s32[16]{0:T(128)} %starts_in.1, bf16[8,32,1024]{2,1,0:T(8,128)(2,1)S(1)} %get-tuple-element.11.q, bf16[8,32,1024]{2,1,0:T(8,128)(2,1)S(1)} %get-tuple-element.12.do, ...), custom_call_target="tpu_custom_call" | custom-call | tf_op jit(solution)/shard_map/attention_grads/pallas_call | solution.py:442
  38.2 26.8 %scatter_grads.1 = (bf16[32,8192]{1,0:T(8,128)(2,1)S(1)}, bf16[32,1024]{1,0:T(8,128)(2,1)S(1)}, bf16[32,1024]{1,0:T(8,128)(2,1)S(1)}) custom-call(bf16[8,32,1024]{2,1,0:T(8,128)(2,1)S(1)} %get-tuple-element.14.dqp, bf16[2,8,2,256,128]{4,3,2,1,0:T(8,128)(2,1)S(1)} %get-tuple-element.15.dkv), custom_call_target="tpu_custom_call" | custom-call | tf_op jit(solution)/shard_map/scatter_grads/pallas_call | solution.py:521
  65.0 0.9 %finish.1 = (bf16[32,8192]{1,0:T(8,128)(2,1)}, bf16[32,1024]{1,0:T(8,128)(2,1)}, bf16[32,1024]{1,0:T(8,128)(2,1)}) custom-call(bf16[32,8192]{1,0:T(8,128)(2,1)S(1)} %get-tuple-element.16.dq_in, bf16[32,1024]{1,0:T(8,128)(2,1)S(1)} %get-tuple-element.17.dk_in, bf16[32,1024]{1,0:T(8,128)(2,1)S(1)} %get-tuple-element.18.dv_in), custom_call_target="tpu_custom_call" | custom-call | tf_op jit(solution)/shard_map/finish/pallas_call | solution.py:566

commit v6 on v5

--- a/solution.py
+++ b/solution.py
@@ -74,7 +74,7 @@
     here = z * PEERS + p
     sibling = y_lo * 2 + 1 - core
     greet(z, p, t, sibling, row)
-    small, large, ring, across, own = {}, [], {}, [], []
+    small, large, own_large, ring, across, own = {}, [], [], {}, [], []
     for part, src in enumerate((k, v)):
         copy = pltpu.make_async_copy(
             src.at[:, pl.ds(pl.multiple_of(p * WIDTH, WIDTH), WIDTH)],
@@ -95,27 +95,6 @@
                 kv_r.at[d, part],
                 (z * PEERS + other, t),
             )
-    wide = HEADS * WIDTH
-    for d in ORDER:
-        other = peer_of(p, d)
-        for part, (src, dst) in enumerate(((q, qg), (do, dog))):
-            large.append(
-                remote(
-                    src.at[:, pl.ds(pl.multiple_of(other * wide, wide), wide)],
-                    dst.at[p],
-                    q_s.at[d, part],
-                    q_r.at[d, part],
-                    (z * PEERS + other, t),
-                )
-            )
-    own_large = []
-    for part, (src, dst) in enumerate(((q, qg), (do, dog))):
-        copy = pltpu.make_async_copy(
-            src.at[:, pl.ds(pl.multiple_of(p * wide, wide), wide)], dst.at[p], q_s.at[0, part]
-        )
-        copy.start()
-        own_large.append(copy)
-
     def piece(part, half, offset):
         return kv.at[core, (z + offset) % RING, part, half_rows(p, half)]
 
@@ -129,6 +108,27 @@
         chunk = piece(part, half, offset)
         key = offset, part, half
         across.append(remote(chunk, chunk, sib_s.at[key], sib_r.at[key], (here, sibling)))
+
+    def send_rows():
+        wide = HEADS * WIDTH
+        for d in ORDER:
+            other = peer_of(p, d)
+            for part, (src, dst) in enumerate(((q, qg), (do, dog))):
+                large.append(
+                    remote(
+                        src.at[:, pl.ds(pl.multiple_of(other * wide, wide), wide)],
+                        dst.at[p],
+                        q_s.at[d, part],
+                        q_r.at[d, part],
+                        (z * PEERS + other, t),
+                    )
+                )
+        for part, (src, dst) in enumerate(((q, qg), (do, dog))):
+            copy = pltpu.make_async_copy(
+                src.at[:, pl.ds(pl.multiple_of(p * wide, wide), wide)], dst.at[p], q_s.at[0, part]
+            )
+            copy.start()
+            own_large.append(copy)
 
     for half in range(2):
         for part in range(2):
@@ -140,6 +140,8 @@
             for way in range(2):
                 forward(0, way, part, half, 0)
             share(part, half, 0)
+        if half == 0:
+            send_rows()
     for step in range(1, 5):
         for half in range(2):
             for part in range(2):
@@ -338,14 +340,17 @@
     sibling = y_lo * 2 + 1 - core
     across, large, ring, small = {}, [], {}, []
     greet(z, p, t, sibling, row)
-    for offset in (4, 3, 5, 2, 6, 1, 7, 0):
-        across[offset] = remote(
-            dkv.at[1 - core, (z + offset) % RING],
-            pair.at[offset],
-            pair_s.at[offset],
-            pair_r.at[offset],
-            (here, sibling),
-        )
+    def exchange(offsets):
+        for offset in offsets:
+            across[offset] = remote(
+                dkv.at[1 - core, (z + offset) % RING],
+                pair.at[offset],
+                pair_s.at[offset],
+                pair_r.at[offset],
+                (here, sibling),
+            )
+
+    exchange((4, 3, 5))
     met = set()
 
     def term(offset, part, half):
@@ -386,6 +391,7 @@
                         value += arrived(3, way, part, half)
                     send(step, way, part, half, value)
         if step == 0:
+            exchange((2, 6, 1, 7, 0))
             pl.semaphore_wait(row, 1)
             wide = HEADS * WIDTH
             columns = pl.ds(pl.multiple_of(p * wide, wide), wide)

time: 65.8 us -> 66.9 us (1.017); the launches traced: 65.8 us -> 65.7 us
    pallas_call x1, Pallas kernels: 8.04 us -> 9.92 us  [attend(): pl.pallas_call(attention_kernel, out_shape=(jax.ShapeDtypeStruct(qg.shape...]
    pallas_call x1, Pallas kernels: 26.8 us -> 24.9 us  [scatter(): pl.pallas_call(scatter_kernel, out_shape=(jax.ShapeDtypeStruct((ROWS, PEE...]
where the time goes in v6:
time: 66.9 us; the launch traced here: 65.7 us
  Pallas kernels  65 us (97%)
    pallas_call x1, Pallas kernels, gather(): pl.pallas_call(gather_kernel, out_shape=(grouped, grouped, chunks), in_sp...  29.3 us
    pallas_call x1, Pallas kernels, scatter(): pl.pallas_call(scatter_kernel, out_shape=(jax.ShapeDtypeStruct((ROWS, PEE...  24.9 us
    pallas_call x1, Pallas kernels, attend(): pl.pallas_call(attention_kernel, out_shape=(jax.ShapeDtypeStruct(qg.shape...  9.92 us

profile of v6, /device:TPU:8, one launch (start us, length us, event | category | flops | bytes accessed | tf_op | source)
XLA Modules:
  0.0 65.7 jit_solution(11534168102809543720)
XLA Ops:
  0.6 29.3 %gather_heads.1 = (bf16[8,32,1024]{2,1,0:T(8,128)(2,1)S(1)}, bf16[8,32,1024]{2,1,0:T(8,128)(2,1)S(1)}, bf16[2,8,2,256,128]{4,3,2,1,0:T(8,128)(2,1)S(1)}) custom-call(bf16[32,8192]{1,0:T(8,128)(2,1)} %q.1, bf16[32,8192]{1,0:T(8,128)(2,1)} %do.1, bf16[32,1024]{1,0:T(8,128)(2,1)} %k.1, bf16[32,1024]{1,0:T(8,128)(2,1)} %v.1), custom_call_target="tpu_custom_call" | custom-call | tf_op jit(solution)/shard_map/gather_heads/pallas_call | solution.py:496
  30.0 9.9 %attention_grads.1 = (bf16[8,32,1024]{2,1,0:T(8,128)(2,1)S(1)}, bf16[2,8,2,256,128]{4,3,2,1,0:T(8,128)(2,1)S(1)}) custom-call(s32[128]{0:T(128)} %spans_in.1, s32[16]{0:T(128)} %starts_in.1, bf16[8,32,1024]{2,1,0:T(8,128)(2,1)S(1)} %get-tuple-element.11.q, bf16[8,32,1024]{2,1,0:T(8,128)(2,1)S(1)} %get-tuple-element.12.do, ...), custom_call_target="tpu_custom_call" | custom-call | tf_op jit(solution)/shard_map/attention_grads/pallas_call | solution.py:448
  39.9 24.9 %scatter_grads.1 = (bf16[32,8192]{1,0:T(8,128)(2,1)S(1)}, bf16[32,1024]{1,0:T(8,128)(2,1)S(1)}, bf16[32,1024]{1,0:T(8,128)(2,1)S(1)}) custom-call(bf16[8,32,1024]{2,1,0:T(8,128)(2,1)S(1)} %get-tuple-element.14.dqp, bf16[2,8,2,256,128]{4,3,2,1,0:T(8,128)(2,1)S(1)} %get-tuple-element.15.dkv), custom_call_target="tpu_custom_call" | custom-call | tf_op jit(solution)/shard_map/scatter_grads/pallas_call | solution.py:527
  64.8 0.9 %finish.1 = (bf16[32,8192]{1,0:T(8,128)(2,1)}, bf16[32,1024]{1,0:T(8,128)(2,1)}, bf16[32,1024]{1,0:T(8,128)(2,1)}) custom-call(bf16[32,8192]{1,0:T(8,128)(2,1)S(1)} %get-tuple-element.16.dq_in, bf16[32,1024]{1,0:T(8,128)(2,1)S(1)} %get-tuple-element.17.dk_in, bf16[32,1024]{1,0:T(8,128)(2,1)S(1)} %get-tuple-element.18.dv_in), custom_call_target="tpu_custom_call" | custom-call | tf_op jit(solution)/shard_map/finish/pallas_call | solution.py:572
